TPU v7x, 128 devices: a whole 4x4x4 slice. The times are simulated.
128 devices in a mesh: dp: 16 (over y, z), cores: 8 (over x, core).
Axes of the slice: x: 4, y: 4, z: 4, core: 2. Of those that a mesh axis runs over, the one named last changes fastest.
Arguments:
- item_digits: int32 [3, 65536], P(None, ('dp', 'cores')), may hold values from 0 to 2047, as said below
- first_core: bfloat16 [2048, 512], replicated, may hold values from -6 to 6
- middle_core: bfloat16 [32768, 512], P(('dp', 'cores')), may hold values from -0.75 to 0.75
- last_core: bfloat16 [1024, 512], replicated, may hold values from -0.75 to 0.75
- w_proj: bfloat16 [512, 2048], replicated, may hold values from -0.25 to 0.25
- w_out: bfloat16 [512, 512], replicated, may hold values from -0.25 to 0.25
- layer_grad: bfloat16 [65536, 512], P(('dp', 'cores')), may hold values from -6 to 6
Outputs:
- layer_out: bfloat16 [65536, 512], P(('dp', 'cores'))
- grad_first: float32 [2048, 512], replicated
- grad_middle: float32 [32768, 512], P(('dp', 'cores'))
- grad_last: float32 [1024, 512], replicated
- grad_proj: float32 [512, 2048], replicated
- grad_out: float32 [512, 512], replicated
Inputs may be any that keep to these rules, and one draw needn't show every extreme that they name: `item_digits`: row 0 lies below 2048, row 1 below 512, row 2 below 1024. An event's owner is its row 1 value divided by 4 (rounded down), the device holding its middle slice. Every history has exactly 8 events of one owner, the same owner for all histories, and its other events spread as evenly as possible over the other owners.
All inputs are finite; a program needn't handle non-finite values.
Results may differ from a plain program's by a relative error of at most 0.017.
Values may be sent and summed in bfloat16 or wider, within the bound.
A program may use at most 192 MiB of HBM per device.

v0:
```python
import math

import jax
import jax.numpy as jnp
from jax import lax
from jax.sharding import PartitionSpec as P

D1 = 8
D2 = 8
D3 = 8
RANK = 64
HEADS = 4
P1 = 2048
P2 = 512
P3 = 1024


def layer_norm(values_in):
    center = values_in - jnp.mean(values_in, axis=-1, keepdims=True)
    spread = jnp.mean(center * center, axis=-1, keepdims=True)
    return center * lax.rsqrt(spread + 1e-05)


def hstu_layer(embedded, w_proj, w_out):
    length = embedded.shape[0]
    row_width = embedded.shape[1]
    head_size = row_width // HEADS
    rows_f = embedded.astype(jnp.float32)
    normed = layer_norm(rows_f).astype(jnp.bfloat16)
    activated = jax.nn.silu(jnp.dot(normed, w_proj, preferred_element_type=jnp.float32))
    gate_u = activated[:, :row_width].astype(jnp.bfloat16)
    values = activated[:, row_width : 2 * row_width].astype(jnp.bfloat16)
    queries = activated[:, 2 * row_width : 3 * row_width].astype(jnp.bfloat16)
    key_heads = activated[:, 3 * row_width :].astype(jnp.bfloat16)
    query_f = queries.astype(jnp.float32).reshape(length, HEADS, head_size)
    key_f = key_heads.astype(jnp.float32).reshape(length, HEADS, head_size)
    value_f = values.astype(jnp.float32).reshape(length, HEADS, head_size)
    scores = jnp.einsum("qhd,khd->hqk", query_f, key_f) * (1.0 / math.sqrt(head_size))
    places = jnp.arange(length, dtype=jnp.int32)
    causal = places[:, None] >= places[None, :]
    attn_weights = jnp.where(causal[None], jax.nn.silu(scores), 0.0).astype(jnp.bfloat16)
    mixed_heads = jnp.einsum("hqk,khd->qhd", attn_weights.astype(jnp.float32), value_f).reshape(
        length, row_width
    )
    gated_rows = (layer_norm(mixed_heads) * gate_u.astype(jnp.float32)).astype(jnp.bfloat16)
    return (jnp.dot(gated_rows, w_out, preferred_element_type=jnp.float32) + rows_f).astype(
        jnp.bfloat16
    )


def per_device(item_digits, first_core, middle_core, last_core, w_proj, w_out, layer_grad):
    events = item_digits.shape[1]
    width_all = layer_grad.shape[1]
    slices = middle_core.shape[0] // RANK
    owners = P2 // slices
    capacity = max(2, 2 * events // owners)
    owner = item_digits[1] // slices
    marks = (owner[:, None] == jnp.arange(owners, dtype=jnp.int32)[None, :]).astype(jnp.int32)
    before = jnp.cumsum(marks, axis=0) - marks
    rank_in = jnp.sum(before * marks, axis=1)
    slot = owner * capacity + rank_in
    outgoing = jnp.full((3, owners * capacity), -1, jnp.int32).at[:, slot].set(item_digits)
    arrived = lax.all_to_all(
        outgoing.reshape(3, owners, capacity),
        ("dp", "cores"),
        split_axis=1,
        concat_axis=1,
        tiled=True,
    ).reshape(3, -1)
    filled = arrived[1] >= 0
    first_index = jnp.where(filled, arrived[0], 0)
    middle_index = jnp.where(filled, arrived[1], 0)
    last_index = jnp.where(filled, arrived[2], 0)
    local_slice = middle_index % slices
    count = arrived.shape[1]
    selector = (
        (local_slice[:, None] == jnp.arange(slices, dtype=jnp.int32)[None, :]) & filled[:, None]
    ).astype(jnp.bfloat16)
    first_rows = first_core[first_index].reshape(count, D1, RANK)
    spread = (selector[:, None, :, None] * first_rows[:, :, None, :]).reshape(
        count * D1, slices * RANK
    )
    partial_rows = jnp.dot(spread, middle_core, preferred_element_type=jnp.float32).astype(
        jnp.bfloat16
    )
    partial_four = partial_rows.reshape(count, D1, D2, RANK)
    last_rows = last_core[last_index].reshape(count, RANK, D3)
    built = (
        jnp.einsum("nabs,nsc->nabc", partial_four, last_rows, preferred_element_type=jnp.float32)
        .reshape(count, width_all)
        .astype(jnp.bfloat16)
    )
    returned = lax.all_to_all(
        built.reshape(owners, capacity, width_all),
        ("dp", "cores"),
        split_axis=0,
        concat_axis=0,
        tiled=True,
    ).reshape(count, width_all)
    embedded = returned[slot]
    layer_rows, pullback = jax.vjp(hstu_layer, embedded, w_proj, w_out)
    row_grad, proj_grad, out_grad = pullback(layer_grad)
    outgoing_grad = jnp.zeros((count, width_all), jnp.bfloat16).at[slot].set(row_grad)
    grad_arrived = lax.all_to_all(
        outgoing_grad.reshape(owners, capacity, width_all),
        ("dp", "cores"),
        split_axis=0,
        concat_axis=0,
        tiled=True,
    ).reshape(count, width_all)
    row_four = grad_arrived.reshape(count, D1, D2, D3)
    partial_grad = jnp.einsum(
        "nabc,nsc->nabs", row_four, last_rows, preferred_element_type=jnp.float32
    ).astype(jnp.bfloat16)
    last_terms = jnp.einsum(
        "nabs,nabc->nsc", partial_four, row_four, preferred_element_type=jnp.float32
    ).reshape(count, RANK * D3)
    last_part = jax.ops.segment_sum(last_terms, last_index, num_segments=P3)
    grad_flat = partial_grad.reshape(count * D1, D2 * RANK)
    grad_middle = lax.dot_general(
        spread, grad_flat, (((0,), (0,)), ((), ())), preferred_element_type=jnp.float32
    )
    spread_grad = lax.dot_general(
        grad_flat, middle_core, (((1,), (1,)), ((), ())), preferred_element_type=jnp.float32
    )
    first_terms = jnp.sum(
        spread_grad.reshape(count, D1, slices, RANK)
        * selector.astype(jnp.float32)[:, None, :, None],
        axis=2,
    )
    first_part = jax.ops.segment_sum(
        first_terms.reshape(count, D1 * RANK), first_index, num_segments=P1
    )
    grad_first, grad_last, proj_total, out_total = lax.psum(
        (first_part, last_part, proj_grad.astype(jnp.float32), out_grad.astype(jnp.float32)),
        ("dp", "cores"),
    )
    return (layer_rows, grad_first, grad_middle, grad_last, proj_total, out_total)


def solution(mesh):
    return jax.shard_map(
        per_device,
        mesh=mesh,
        in_specs=(
            P(None, ("dp", "cores")),
            P(),
            P(("dp", "cores"), None),
            P(),
            P(),
            P(),
            P(("dp", "cores"), None),
        ),
        out_specs=(P(("dp", "cores"), None), P(), P(("dp", "cores"), None), P(), P(), P()),
        check_vma=False,
    )
```

profile of v0, /device:TPU:1, one launch (start us, length us, event | category | flops | bytes accessed | tf_op | source)
XLA Modules:
  0.0 534.6 jit_solution(2522201154714991266)
XLA Ops:
  7.2 0.9 slice.38
  10.3 1.8 scatter_custom_fusion
  13.0 22.9 %all_to_all.15 = s32[3,128,8]{2,0,1:T(4,128)S(1)} all-to-all(s32[3,128,8]{2,0,1:T(4,128)S(1)} %copy.67), channel_id=1, replica_groups=mesh['dp'=16,'cores'=8] {'dp','cores'}, dimensions={1} | all-to-all | bytes 24576 | tf_op jit(solution)/shard_map/all_to_all | solution.py:63
  36.4 1.6 fusion.56
  39.1 5.9 %gather_fusion = bf16[1024,512]{1,0:T(8,128)(2,1)S(1)} fusion(bf16[2048,512]{1,0:T(8,128)(2,1)} %param.8, s32[1024]{0:T(1024)S(1)} %broadcast_clamp_fusion.1), kind=kCustom, calls=%fused_computation | custom fusion | bytes 2101248 | tf_op jit(solution)/shard_map/gather | solution.py:79
  45.0 1.3 copy.69
  46.3 3.5 copy.70
  49.7 7.0 %broadcast_multiply_fusion = bf16[1024,8,4,64]{3,2,1,0:T(4,128)(2,1)} fusion(bf16[1024,8,64]{2,1,0:T(8,128)(2,1)} %copy.70, bf16[1024,4]{1,0:T(8,128)(2,1)S(1)} %copy.68), kind=kLoop, calls=%fused_computation.22 | loop fusion | flops 2097152 | bytes 5251072 | tf_op jit(solution)/shard_map/mul | solution.py:80
  56.7 12.7 %mul.185 = bf16[8192,256]{1,0:T(8,128)(2,1)} reshape(bf16[1024,8,4,64]{3,2,1,0:T(4,128)(2,1)} %broadcast_multiply_fusion) | data formatting | bytes 8388608 | tf_op jit(solution)/shard_map/mul | solution.py:80
  69.5 7.8 %convolution_convert_fusion = bf16[8192,512]{1,0:T(8,128)(2,1)} fusion(bf16[8192,256]{1,0:T(8,128)(2,1)} %mul.185, bf16[256,512]{1,0:T(8,128)(2,1)S(1)} %copy-done.24), kind=kOutput, calls=%fused_computation.7 | convolution fusion | flops 2151677952 | bytes 12845056 | tf_op jit(solution)/shard_map/dot_general | solution.py:83
  77.2 21.3 %reshape.442 = bf16[1024,8,8,64]{3,2,1,0:T(8,128)(2,1)} reshape(bf16[8192,512]{1,0:T(8,128)(2,1)} %convolution_convert_fusion) | data formatting | bytes 16777216 | tf_op jit(solution)/shard_map/reshape | solution.py:86
  98.5 0.9 select_n.123
  99.5 5.1 gather_fusion.1
  104.6 1.5 copy.71
  106.1 3.0 copy.94
  109.1 13.9 %convolution_convert_fusion.2 = bf16[1024,8,8,8]{3,2,1,0:T(8,128)(2,1)} fusion(bf16[1024,8,8,64]{3,2,1,0:T(8,128)(2,1)} %reshape.442, bf16[1024,64,8,1]{1,2,3,0:T(8,128)(2,1)} %copy.94), kind=kOutput, calls=%fused_computation.9 | convolution fusion | flops 67633152 | bytes 10485760 | tf_op jit(solution)/shard_map/nabs,nsc->nabc/dot_general | solution.py:89
  123.0 25.2 %convert_element_type.144 = bf16[128,8,512]{2,1,0:T(8,128)(2,1)} reshape(bf16[1024,8,8,8]{3,2,1,0:T(8,128)(2,1)} %convolution_convert_fusion.2) | data formatting | bytes 2097152 | tf_op jit(solution)/shard_map/convert_element_type | solution.py:91
  148.2 4.7 all-to-all-start.1
  153.8 18.4 %all-to-all-done.1 = bf16[128,8,512]{2,1,0:T(8,128)(2,1)S(1)} async-done(((bf16[128,8,512]{2,1,0:T(8,128)(2,1)}), bf16[128,8,512]{2,1,0:T(8,128)(2,1)S(1)}, u32[]{:S(2)}, u32[]{:S(2)}) %all-to-all-start.1) | async-done | bytes 1048608 | tf_op jit(solution)/shard_map/all_to_all | solution.py:93
  172.2 2.6 gather_fusion.2
  174.9 1.2 convert_reduce_fusion
  176.1 1.3 fusion.16
  177.4 4.7 multiply_convert_fusion
  182.1 1.3 copy-done.12
  183.5 1.2 slice_bitcast_fusion
  184.9 1.4 copy.114
  186.3 4.7 select_convert_fusion
  191.1 1.3 copy-done.5
  194.0 1.3 copy.104
  195.3 2.3 multiply_reduce_fusion.1
  198.3 3.0 fusion.55
  201.5 1.0 copy.105
  202.5 4.4 fusion.2
  207.4 1.6 fusion.61
  209.1 1.2 fusion.60
  210.5 2.1 copy.107
  212.6 2.0 copy.108
  214.6 3.7 fusion.4
  218.4 1.5 fusion.18
  221.2 4.3 scatter_custom_fusion.1
  225.6 5.3 all-to-all-start.2
  231.1 2.5 fusion.12
  233.6 3.5 fusion.5
  237.1 12.9 %all-to-all-done.2 = bf16[128,8,512]{2,1,0:T(8,128)(2,1)} async-done(((bf16[128,8,512]{2,1,0:T(8,128)(2,1)}), bf16[128,8,512]{2,1,0:T(8,128)(2,1)}, u32[]{:S(2)}, u32[]{:S(2)}) %all-to-all-start.2) | async-done | bytes 1048608 | tf_op jit(solution)/shard_map/all_to_all | solution.py:104
  250.0 22.3 %reshape_reshape.3 = bf16[1024,8,8,8]{3,2,1,0:T(8,128)(2,1)} reshape(bf16[128,8,512]{2,1,0:T(8,128)(2,1)} %all-to-all-done.2) | data formatting | bytes 2097152 | tf_op jit(solution)/shard_map/reshape;reshape | solution.py:111
  272.3 14.6 %convolution_bitcast_fusion = f32[1024,64,8]{1,2,0:T(8,128)} fusion(bf16[1024,8,8,64]{3,2,1,0:T(8,128)(2,1)} %reshape.442, bf16[1024,8,8,8]{3,2,1,0:T(8,128)(2,1)} %reshape_reshape.3), kind=kOutput, calls=%fused_computation.25 | convolution fusion | flops 67108864 | bytes 11534336 | tf_op jit(solution)/shard_map/nabs,nabc->nsc/dot_general | solution.py:115
  287.0 14.6 %convolution_convert_fusion.1 = bf16[1024,8,8,64]{3,2,1,0:T(8,128)(2,1)} fusion(bf16[1024,8,8,8]{3,2,1,0:T(8,128)(2,1)} %reshape_reshape.3, bf16[1024,64,8,1]{1,2,3,0:T(8,128)(2,1)S(1)} %copy-done.4), kind=kOutput, calls=%fused_computation.8 | convolution fusion | flops 71303168 | bytes 10485760 | tf_op jit(solution)/shard_map/nabc,nsc->nabs/dot_general | solution.py:112
  301.6 3.7 copy.92
  305.3 1.8 copy.93
  307.1 18.3 %copy.88 = bf16[1024,8,8,64]{0,3,2,1:T(8,128)(2,1)} copy(bf16[1024,8,8,64]{3,2,1,0:T(8,128)(2,1)} %convolution_convert_fusion.1) | data formatting | bytes 16777216 | tf_op jit(solution)/shard_map/convert_element_type | solution.py:114
  325.4 8.2 %multiply_reduce_fusion = f32[1024,8,64]{0,2,1:T(8,128)} fusion(f32[1024,4]{0,1:T(4,128)S(1)} %copy-done.25, bf16[1024,8,512,1]{0,2,3,1:T(8,128)(2,1)} %bitcast.124, bf16[4,64,512,1]{2,1,0,3:T(8,128)(2,1)S(1)} %bitcast.142), kind=kOutput, calls=%fused_computation.10 | convolution fusion | flops 2151153664 | bytes 10764288 | tf_op jit(solution)/shard_map/dot_general | solution.py:123
  333.7 1.9 copy.90
  335.6 8.8 %scatter_custom_fusion.3 = f32[1024,512]{1,0:T(8,128)} fusion(s32[1024]{0:T(1024)S(1)} %reshape.504, f32[1024,512]{1,0:T(8,128)} %copy.93, f32[]{:T(128)} %constant.66.clone.1), kind=kCustom, calls=%fused_computation.57 | custom fusion | flops 524288 | bytes 2097664 | tf_op jit(solution)/shard_map/scatter-add | solution.py:118
  344.4 8.8 %scatter_custom_fusion.2 = f32[2048,512]{1,0:T(8,128)} fusion(s32[1024]{0:T(1024)S(1)} %reshape.496, f32[1024,512]{1,0:T(8,128)S(1)} %copy.90, f32[]{:T(128)} %constant.66.clone.1), kind=kCustom, calls=%fused_computation.26 | custom fusion | flops 524288 | bytes 4194308 | tf_op jit(solution)/shard_map/scatter-add | solution.py:131
  353.3 1.0 copy-done.10
  354.4 1.2 fusion.13
  355.7 22.9 %reshape.452 = bf16[8192,512]{1,0:T(8,128)(2,1)} reshape(bf16[1024,8,8,64]{3,2,1,0:T(8,128)(2,1)} %convolution_convert_fusion.1) | data formatting | bytes 16777216 | tf_op jit(solution)/shard_map/reshape | solution.py:119
  378.6 8.3 %fusion.59 = f32[256,512]{1,0:T(8,128)} fusion(bf16[8192,256]{1,0:T(8,128)(2,1)} %mul.185, bf16[8192,512]{1,0:T(8,128)(2,1)} %reshape.452), kind=kOutput, calls=%fused_computation.140 | convolution fusion | flops 2147483648 | bytes 13107200 | tf_op jit(solution)/shard_map/dot_general | solution.py:120
  386.9 130.0 %all-reduce.7.cloned.1.call-done = (f32[2048,512]{1,0:T(8,128)}, f32[1024,512]{1,0:T(8,128)}, f32[512,2048]{1,0:T(8,128)}, f32[512,512]{1,0:T(8,128)}) async-done(((f32[2048,512]{1,0:T(8,128)}, f32[1024,512]{1,0:T(8,128)}, f32[512,2048]{1,0:T(8,128)}, f32[512,512]{1,0:T(8,128)}), (f32[2048,512]{1,0:T(8,128)}, f32[1024,512]{1,0:T(8,128)}, f32[512,2048]{1,0:T(8,128)}, ...) | async-done | bytes 11534352 | tf_op jit(solution)/shard_map/psum | solution.py:134
  516.9 4.8 copy.130
  521.7 1.3 copy.131
  523.0 1.6 copy-done.11
  524.6 2.0 copy.132
  526.6 1.0 copy.133
  (95 shorter events, 10.6 us)
Async XLA Ops:
  7.2 170.2 %copy-start = (bf16[512,2048]{1,0:T(8,128)(2,1)S(1)}, bf16[512,2048]{1,0:T(8,128)(2,1)}, u32[]{:S(2)}) copy-start(bf16[512,2048]{1,0:T(8,128)(2,1)} %param.11) | copy-start | bytes 6291460
  9.4 143.6 %copy-start.26 = (s32[512,1]{0,1:T(1,128)}, s32[512,1]{0,1:T(1,128)S(1)}, u32[]{:S(2)}) copy-start(s32[512,1]{0,1:T(1,128)S(1)} %compare_select_fusion.4) | copy-start | bytes 6148
  56.7 12.8 %copy-start.24 = (bf16[256,512]{1,0:T(8,128)(2,1)S(1)}, bf16[256,512]{1,0:T(8,128)(2,1)}, u32[]{:S(2)}) copy-start(bf16[256,512]{1,0:T(8,128)(2,1)} %param.9) | copy-start | bytes 786436
  77.2 22.3 %copy-start.2 = (bf16[1024,512]{1,0:T(8,128)(2,1)S(1)}, bf16[1024,512]{1,0:T(8,128)(2,1)}, u32[]{:S(2)}) copy-start(bf16[1024,512]{1,0:T(8,128)(2,1)} %param.10) | copy-start | bytes 3145732
  148.2 24.0 %all-to-all-start.1 = ((bf16[128,8,512]{2,1,0:T(8,128)(2,1)}), bf16[128,8,512]{2,1,0:T(8,128)(2,1)S(1)}, u32[]{:S(2)}, u32[]{:S(2)}) async-start(bf16[128,8,512]{2,1,0:T(8,128)(2,1)} %convert_element_type.144), calls=%async_computation.1 | async-start | bytes 2097152 | tf_op jit(solution)/shard_map/all_to_all | solution.py:93
  182.1 1.3 copy-start.12
  184.8 6.2 %copy-start.16 = (bf16[512,512]{0,1:T(8,128)(2,1)}, bf16[512,512]{0,1:T(8,128)(2,1)S(1)}, u32[]{:S(2)}) copy-start(bf16[512,512]{0,1:T(8,128)(2,1)S(1)} %copy.113) | copy-start | bytes 1572868
  186.3 4.8 copy-start.18
  186.3 6.1 %copy-start.14 = (bf16[64,4,8,128]{3,2,1,0:T(8,128)(2,1)S(1)}, bf16[64,4,8,128]{3,2,1,0:T(8,128)(2,1)}, u32[]{:S(2)}) copy-start(bf16[64,4,8,128]{3,2,1,0:T(8,128)(2,1)} %get-tuple-element.17) | copy-start | bytes 1572868
  191.1 1.3 copy-start.5
  197.6 4.9 copy-start.15
  202.5 4.4 copy-start.17
  202.5 4.9 copy-start.19
  206.9 2.1 copy-start.6
  206.9 2.1 copy-start.20
  214.6 3.8 copy-start.3
  218.4 1.5 copy-start.7
  218.4 2.8 copy-start.9
  219.9 0.8 copy-start.21
  219.9 13.7 %copy-start.8 = (bf16[512,2048]{1,0:T(8,128)(2,1)S(1)}, bf16[512,2048]{1,0:T(8,128)(2,1)}, u32[]{:S(2)}) copy-start(bf16[512,2048]{1,0:T(8,128)(2,1)} %copy-done.7) | copy-start | bytes 6291460
  225.6 24.5 %all-to-all-start.2 = ((bf16[128,8,512]{2,1,0:T(8,128)(2,1)}), bf16[128,8,512]{2,1,0:T(8,128)(2,1)}, u32[]{:S(2)}, u32[]{:S(2)}) async-start(bf16[128,8,512]{2,1,0:T(8,128)(2,1)} %bitcast.128), calls=%async_computation.2 | async-start | bytes 2097152 | tf_op jit(solution)/shard_map/all_to_all | solution.py:104
  230.9 286.0 %all-reduce.7.cloned.1.call-start = ((), (), s32[]{:S(2)}) async-start(), calls=%async_computation.3 | async-start | bytes 23068672 | tf_op jit(solution)/shard_map/psum | solution.py:134
  272.3 14.7 %copy-start.4 = (bf16[1024,64,8,1]{1,2,3,0:T(8,128)(2,1)S(1)}, bf16[1024,64,8,1]{1,2,3,0:T(8,128)(2,1)}, u32[]{:S(2)}) copy-start(bf16[1024,64,8,1]{1,2,3,0:T(8,128)(2,1)} %copy.94) | copy-start | bytes 3145732
  307.1 18.3 %copy-start.25 = (f32[1024,4]{0,1:T(4,128)S(1)}, f32[1024,4]{0,1:T(4,128)}, u32[]{:S(2)}) copy-start(f32[1024,4]{0,1:T(4,128)} %get-tuple-element.24) | copy-start | bytes 49156
  353.2 1.0 copy-start.10
  353.2 1.2 copy-start.22
  516.9 4.8 copy-start.13
  521.7 2.9 copy-start.11
  521.7 5.9 %copy-start.1 = (bf16[512,2048]{1,0:T(8,128)(2,1)S(1)}, bf16[512,2048]{1,0:T(8,128)(2,1)}, u32[]{:S(2)}) copy-start(bf16[512,2048]{1,0:T(8,128)(2,1)} %param.11) | copy-start | bytes 6291460
  524.6 2.0 copy-start.23
Sparse Core Ops, SparseCore 0:
  353.4 163.4 all-reduce.6
where the time goes:
time: 540 us; the launch traced here: 535 us
  local copies, waits for them, and re-layouts  184 us (34%)
  waiting for transfers between devices  161 us (30%)
  matrix products  96.4 us (18%)
  other arithmetic  44.7 us (8%)
  blocking collectives  22.9 us (4%)
  between operations  14.6 us (3%)
  starting transfers between devices  10.1 us (2%)
    psum x1, waiting for transfers between devices, per_device(): lax.psum((first_part, last_part, proj_grad.astype(jnp.float32), out_grad....  130 us
    convert_element_type x1, local copies, waits for them, and re-layouts, per_device(): built = jnp.einsum('nabs,nsc->nabc', partial_four, last_rows, preferred_e...  25.2 us
    reshape x1, local copies, waits for them, and re-layouts, per_device(): grad_flat = partial_grad.reshape(count * D1, D2 * RANK)  22.9 us
    all_to_all x1, blocking collectives, per_device(): lax.all_to_all(outgoing.reshape(3, owners, capacity), ('dp', 'cores'), sp...  22.9 us
    another operation x1, local copies, waits for them, and re-layouts, per_device(): row_four = grad_arrived.reshape(count, D1, D2, D3)  22.3 us
    reshape x1, local copies, waits for them, and re-layouts, per_device(): partial_four = partial_rows.reshape(count, D1, D2, RANK)  21.3 us
    all_to_all x1, waiting for transfers between devices, per_device(): lax.all_to_all(built.reshape(owners, capacity, width_all), ('dp', 'cores'...  18.4 us
    convert_element_type x1, local copies, waits for them, and re-layouts, per_device(): partial_grad = jnp.einsum('nabc,nsc->nabs', row_four, last_rows, preferre...  18.3 us
  transfers between devices with their start and end apart: 3, of which 3 were waited for; matrix products, arithmetic and copies ran while one was open for 7% of the time, Pallas kernels for 0%

commit v1 on v0

v1 whole, which is shorter than its diff:
```python
import functools
import math

import jax
import jax.numpy as jnp
from jax import lax
from jax.experimental import pallas as pl
from jax.experimental.pallas import tpu as pltpu
from jax.sharding import PartitionSpec as P

AXES = ("dp", "cores")
BF = jnp.bfloat16
F32 = jnp.float32
I32 = jnp.int32
EVENTS = 512
OWNERS = 128
VMEM_LIMIT = 56 * 1024 * 1024


def iota(shape, dim):
    return lax.broadcasted_iota(I32, shape, dim)


def dot(a, b, ca=1, cb=0):
    return lax.dot_general(a, b, (((ca,), (cb,)), ((), ())), preferred_element_type=F32)


def bdot(a, b, ca, cb):
    return lax.dot_general(a, b, (((ca,), (cb,)), ((0,), (0,))), preferred_element_type=F32)


def half_turn(x):
    return pltpu.roll(x, 64, x.ndim - 1)


def low_lanes(shape):
    return iota(shape, len(shape) - 1) % 128 < 64


def one_hot(flag):
    return jnp.where(flag, 1.0, 0.0).astype(BF)


def prep_kernel(dig_ref, msg_ref, slot_row_ref, slot_col_ref):
    digits = dig_ref[...]
    padded = jnp.concatenate([digits, jnp.zeros((5, EVENTS), I32)], axis=0).astype(F32)
    cols = jnp.transpose(padded).astype(I32)
    owner_row = digits[1:2, :] >> 2
    owner_col = cols[:, 1:2] >> 2
    same = owner_row == owner_col
    sub = iota((EVENTS, EVENTS), 0)
    lane = iota((EVENTS, EVENTS), 1)
    rank_col = jnp.sum(jnp.where(same & (lane < sub), 1.0, 0.0), axis=1, keepdims=True).astype(I32)
    rank_row = jnp.sum(jnp.where(same & (sub < lane), 1.0, 0.0), axis=0, keepdims=True).astype(I32)
    slot_row_ref[...] = jnp.broadcast_to(rank_row * OWNERS + owner_row, (8, EVENTS))
    slot_col_ref[...] = jnp.broadcast_to(rank_col * OWNERS + owner_col, (EVENTS, 128))
    place = iota((EVENTS, 128), 1)
    inner = place % 32
    value = jnp.where(inner < 8, cols[:, 0:1], jnp.where(inner < 16, cols[:, 1:2], cols[:, 2:3])) + 1
    part = jnp.where(place < 32, value >> 4, value & 15)
    ok = (inner % 8 == rank_col) & (inner < 24) & (place < 64)
    table = jnp.where(ok, part, 0).astype(F32).astype(BF)
    pick = one_hot(iota((OWNERS, EVENTS), 0) == owner_row)
    sums = dot(pick, table)
    whole = sums * 16.0 + pltpu.roll(sums, 96, 1)
    msg_ref[...] = jnp.where(iota((OWNERS, 128), 1) < 24, whole, 0.0).astype(I32).reshape(OWNERS, 1, 128)


def prep(digits):
    return pl.pallas_call(
        prep_kernel,
        out_shape=(
            jax.ShapeDtypeStruct((OWNERS, 1, 128), I32),
            jax.ShapeDtypeStruct((8, EVENTS), I32),
            jax.ShapeDtypeStruct((EVENTS, 128), I32),
        ),
        compiler_params=pltpu.CompilerParams(vmem_limit_bytes=VMEM_LIMIT),
        name="prep",
    )(digits)


def index_columns(arrived, half):
    lane = iota((OWNERS, 128), 1)
    out = []
    for digit in range(3):
        parts = []
        for t in range(4):
            mine = lane == digit * 8 + half * 4 + t
            parts.append(jnp.sum(jnp.where(mine, arrived, 0).astype(F32), axis=1, keepdims=True))
        out.append(jnp.concatenate(parts, axis=0).astype(I32) - 1)
    return out


def slice_masks(middle_col):
    local = jnp.where(middle_col < 0, -1, middle_col & 3)
    group = iota((512, 128), 1) // 64
    return local == group, local == group + 2


def build_kernel(arrived_ref, first_ref, middle_ref, last_ref, built_ref, spread_ref, part_ref, lt_ref, fs, ps, ls):
    half = pl.program_id(0)
    arrived = arrived_ref[...].reshape(OWNERS, 128)
    first_col, middle_col, last_col = index_columns(arrived, half)
    low = low_lanes((128, 128))
    rows = dot(one_hot(first_col == iota((512, 2048), 1)), first_ref[...])
    mask0, mask1 = slice_masks(middle_col)
    for t in range(4):
        m0 = mask0[t * 128 : (t + 1) * 128]
        m1 = mask1[t * 128 : (t + 1) * 128]
        for pair in range(4):
            x = rows[t * 128 : (t + 1) * 128, pair * 128 : (pair + 1) * 128]
            turned = half_turn(x)
            for odd in range(2):
                both = jnp.where(low, turned, x) if odd else jnp.where(low, x, turned)
                at = pl.ds(t * 1024 + pair * 2 + odd, 128, stride=8)
                fs[0, at, :] = jnp.where(m0, both, 0.0)
                fs[1, at, :] = jnp.where(m1, both, 0.0)
    source = iota((512, 512), 0)
    perm = one_hot(iota((512, 512), 1) == (source % 8) * 64 + source // 8)
    rows = dot(one_hot(last_col == iota((512, 1024), 1)), last_ref[...]).astype(BF)
    rows = dot(rows, perm)
    for t in range(4):
        for pair in range(4):
            x = rows[t * 128 : (t + 1) * 128, pair * 128 : (pair + 1) * 128]
            turned = half_turn(x)
            for odd in range(2):
                both = jnp.where(low, turned, x) if odd else jnp.where(low, x, turned)
                keep = jnp.where(low, 0.0, both) if t % 2 else jnp.where(low, both, 0.0)
                ls[t // 2, pl.ds((t % 2) * 8 + pair * 2 + odd, 128, stride=16), :] = keep

    def spread_step(i, carry):
        at = pl.ds(pl.multiple_of(i * 512, 512), 512)
        spread_ref[at, 0:128] = fs[0, at, :].astype(BF)
        spread_ref[at, 128:256] = fs[1, at, :].astype(BF)
        ps[at, :] = dot(spread_ref[at, :], middle_ref[...])
        return carry

    lax.fori_loop(0, 8, spread_step, 0)

    group = 16
    low = low_lanes((group * 8, 128))

    def combine(i, carry):
        srcs = pl.ds(pl.multiple_of(i * group, group), group)
        for pair in range(4):
            lanes = slice(pair * 128, (pair + 1) * 128)
            v = [ps[pl.ds(pl.multiple_of(t * 1024 + i * group * 8, 8), group * 8), lanes] for t in range(4)]
            w = [half_turn(x) for x in v]
            for side in range(2):
                v0, v1 = v[2 * side], v[2 * side + 1]
                w0, w1 = w[2 * side], w[2 * side + 1]
                even = jnp.where(low, v0, w1).reshape(group, 8, 128)
                odd = jnp.where(low, w0, v1).reshape(group, 8, 128)
                part_ref[srcs, pair * 16 : (pair + 1) * 16, side * 128 : (side + 1) * 128] = jnp.concatenate(
                    [even, odd], axis=1
                ).astype(BF)
        wide = pl.ds(pl.multiple_of(i * group * 16, group * 16), group * 16)
        zero = jnp.zeros((group, 16, 128), BF)
        lt_ref[srcs, 0:16, 0:128] = ls[0, wide, :].reshape(group, 16, 128).astype(BF)
        lt_ref[srcs, 0:16, 128:256] = zero
        lt_ref[srcs, 16:32, 0:128] = zero
        lt_ref[srcs, 16:32, 128:256] = ls[1, wide, :].reshape(group, 16, 128).astype(BF)
        out = bdot(lt_ref[srcs], part_ref[srcs], 2, 2)
        tile = jnp.concatenate([out[:, 0:16, :], out[:, 16:32, :]], axis=2)
        built_ref[srcs, 0] = tile.astype(BF)
        return carry

    lax.fori_loop(0, OWNERS // group, combine, 0)


def build(arrived, first_core, middle_core, last_core):
    return pl.pallas_call(
        build_kernel,
        grid=(2,),
        in_specs=[
            pl.BlockSpec((OWNERS, 1, 128), lambda h: (0, 0, 0)),
            pl.BlockSpec((2048, 512), lambda h: (0, 0)),
            pl.BlockSpec((256, 512), lambda h: (0, 0)),
            pl.BlockSpec((1024, 512), lambda h: (0, 0)),
        ],
        out_specs=(
            pl.BlockSpec((OWNERS, 1, 16, 128), lambda h: (0, h, 0, 0)),
            pl.BlockSpec((4096, 256), lambda h: (h, 0)),
            pl.BlockSpec((OWNERS, 64, 256), lambda h: (h, 0, 0)),
            pl.BlockSpec((OWNERS, 32, 256), lambda h: (h, 0, 0)),
        ),
        out_shape=(
            jax.ShapeDtypeStruct((OWNERS, 2, 16, 128), BF),
            jax.ShapeDtypeStruct((8192, 256), BF),
            jax.ShapeDtypeStruct((2 * OWNERS, 64, 256), BF),
            jax.ShapeDtypeStruct((2 * OWNERS, 32, 256), BF),
        ),
        scratch_shapes=[
            pltpu.VMEM((2, 4096, 128), F32),
            pltpu.VMEM((4096, 512), F32),
            pltpu.VMEM((2, 2048, 128), F32),
        ],
        compiler_params=pltpu.CompilerParams(vmem_limit_bytes=VMEM_LIMIT),
        name="build",
    )(arrived, first_core, middle_core, last_core)


def sigmoid(x):
    return 1.0 / (1.0 + jnp.exp(-x))


def norm_stats(x):
    center = x - jnp.mean(x, axis=-1, keepdims=True)
    spread = jnp.mean(center * center, axis=-1, keepdims=True)
    scale = lax.rsqrt(spread + 1e-05)
    return center * scale, scale


def norm_grad(ct, y, scale):
    return scale * (ct - jnp.mean(ct, axis=-1, keepdims=True) - y * jnp.mean(ct * y, axis=-1, keepdims=True))


def layer_kernel(
    recv_ref, slot_row_ref, slot_col_ref, proj_ref, out_ref, grad_ref,
    rows_ref, sent_ref, dproj_ref, dout_ref,
    tiles, slots, emb, normed, y_in, z, act, mixed, y_mid, gated, dz, dmixed, work, sc_in, sc_mid,
):
    low = low_lanes((256 // 2, 128))
    step = 128

    def widen(i, carry):
        srcs = pl.ds(pl.multiple_of(i * 32, 32), 32)
        tiles[pl.ds(pl.multiple_of(i * 1024, 1024), 1024), :] = recv_ref[srcs].reshape(1024, 128).astype(F32)
        return carry

    lax.fori_loop(0, 4, widen, 0)
    for half in range(2):
        for tlo in range(2):
            for pair in range(4):
                base = half * 16 + tlo * 8 + pair * 2
                y0 = tiles[pl.ds(base, 128, stride=32), :]
                y1 = tiles[pl.ds(base + 1, 128, stride=32), :]
                lanes = slice(pair * 128, (pair + 1) * 128)
                k0 = half * 4 + tlo
                slots[k0 * 128 : (k0 + 1) * 128, lanes] = jnp.where(low, y0, half_turn(y1)).astype(BF)
                k1 = k0 + 2
                slots[k1 * 128 : (k1 + 1) * 128, lanes] = jnp.where(low, half_turn(y0), y1).astype(BF)
    source = iota((512, 512), 0)
    target = iota((512, 512), 1)
    flip = one_hot(target == (source % 8) * 64 + ((source // 8) % 8) * 8 + source // 64)
    pick = one_hot(slot_col_ref[:, 0:1] == iota((EVENTS, 1024), 1))
    emb[...] = dot(dot(pick, slots[...]).astype(BF), flip)

    def project(i, carry):
        at = pl.ds(pl.multiple_of(i * step, step), step)
        y, scale = norm_stats(emb[at, :])
        y_in[at, :] = y
        sc_in[at, :] = jnp.broadcast_to(scale, (step, 128))
        normed[at, :] = y.astype(BF)
        for block in range(4):
            lanes = slice(block * 512, (block + 1) * 512)
            value = dot(normed[at, :], proj_ref[:, lanes])
            z[at, lanes] = value
            act[at, lanes] = (value * sigmoid(value)).astype(BF)
        return carry

    lax.fori_loop(0, EVENTS // step, project, 0)
    scaling = 1.0 / math.sqrt(128.0)

    def scores_of(head, rows, base):
        q = act[rows, pl.ds(pl.multiple_of(1024 + head * 128, 128), 128)]
        k = act[:, pl.ds(pl.multiple_of(1536 + head * 128, 128), 128)]
        s = dot(q, k, 1, 1) * scaling
        causal = base + iota((step, EVENTS), 0) >= iota((step, EVENTS), 1)
        return s, causal

    def attend(j, carry):
        head = j // 4
        base = pl.multiple_of((j % 4) * step, step)
        rows = pl.ds(base, step)
        cols = pl.ds(pl.multiple_of(head * 128, 128), 128)
        s, causal = scores_of(head, rows, base)
        weights = jnp.where(causal, s * sigmoid(s), 0.0).astype(BF)
        v = act[:, pl.ds(pl.multiple_of(512 + head * 128, 128), 128)]
        mixed[rows, cols] = dot(weights, v)
        return carry

    lax.fori_loop(0, 16, attend, 0)

    def finish(i, carry):
        at = pl.ds(pl.multiple_of(i * step, step), step)
        y, scale = norm_stats(mixed[at, :])
        u = act[at, 0:512].astype(F32)
        gate = (y * u).astype(BF)
        gated[at, :] = gate
        g = grad_ref[at, :]
        rows_ref[at, :] = (dot(gate, out_ref[...]) + emb[at, :]).astype(BF)
        d_gate = dot(g, out_ref[...], 1, 1).astype(BF).astype(F32)
        d_u = (d_gate * y).astype(BF).astype(F32)
        zu = z[at, 0:512]
        sig = sigmoid(zu)
        dz[at, 0:512] = (d_u * (sig * (1.0 + zu * (1.0 - sig)))).astype(BF)
        dmixed[at, :] = norm_grad(d_gate * u, y, scale).astype(BF)
        return carry

    lax.fori_loop(0, EVENTS // step, finish, 0)
    dout_ref[...] = dot(gated[...], grad_ref[...], 0, 0).astype(BF)

    def attend_grad(head, carry):
        cols = pl.ds(pl.multiple_of(head * 128, 128), 128)
        vcols = pl.ds(pl.multiple_of(512 + head * 128, 128), 128)
        qcols = pl.ds(pl.multiple_of(1024 + head * 128, 128), 128)
        kcols = pl.ds(pl.multiple_of(1536 + head * 128, 128), 128)
        d_v = jnp.zeros((EVENTS, 128), F32)
        d_k = jnp.zeros((EVENTS, 128), F32)
        for block in range(4):
            base = block * step
            rows = slice(base, base + step)
            s, causal = scores_of(head, rows, base)
            sig = sigmoid(s)
            weights = jnp.where(causal, s * sig, 0.0).astype(BF)
            dm = dmixed[rows, cols]
            d_w = dot(dm, act[:, vcols], 1, 1).astype(BF).astype(F32)
            d_s = jnp.where(causal, d_w * (sig * (1.0 + s * (1.0 - sig))) * scaling, 0.0).astype(BF)
            d_v += dot(weights, dm, 0, 0)
            d_k += dot(d_s, act[rows, qcols], 0, 0)
            d_q = dot(d_s, act[:, kcols])
            work[rows, :] = d_q

        def through(ct, where):
            value = z[:, where]
            sig = sigmoid(value)
            dz[:, where] = (ct.astype(BF).astype(F32) * (sig * (1.0 + value * (1.0 - sig)))).astype(BF)

        through(work[...], qcols)
        through(d_v, vcols)
        through(d_k, kcols)
        return carry

    lax.fori_loop(0, 4, attend_grad, 0)

    for block in range(4):
        lanes = slice(block * 512, (block + 1) * 512)
        dproj_ref[:, lanes] = dot(normed[...], dz[:, lanes], 0, 0).astype(BF)

    back = one_hot(source == (target % 8) * 64 + ((target // 8) % 8) * 8 + target // 64)

    def close(i, carry):
        at = pl.ds(pl.multiple_of(i * step, step), step)
        d_normed = dot(dz[at, :], proj_ref[...], 1, 1).astype(BF).astype(F32)
        d_rows = norm_grad(d_normed, y_in[at, :], sc_in[at, 0:1]) + grad_ref[at, :].astype(F32)
        gated[at, :] = d_rows.astype(BF)
        return carry

    lax.fori_loop(0, EVENTS // step, close, 0)
    turned = dot(gated[...], back).astype(BF)
    for half in range(2):
        for tlo in range(2):
            found = []
            for thi in range(2):
                k = half * 4 + thi * 2 + tlo
                place = one_hot(iota((128, EVENTS), 0) + k * 128 == slot_row_ref[0:1, :])
                found.append(dot(place, turned))
            for pair in range(4):
                lanes = slice(pair * 128, (pair + 1) * 128)
                x0, x1 = found[0][:, lanes], found[1][:, lanes]
                base = half * 16 + tlo * 8 + pair * 2
                tiles[pl.ds(base, 128, stride=32), :] = jnp.where(low, x0, half_turn(x1))
                tiles[pl.ds(base + 1, 128, stride=32), :] = jnp.where(low, half_turn(x0), x1)

    def narrow(i, carry):
        srcs = pl.ds(pl.multiple_of(i * 32, 32), 32)
        sent_ref[srcs] = tiles[pl.ds(pl.multiple_of(i * 1024, 1024), 1024), :].astype(BF).reshape(32, 2, 16, 128)
        return carry

    lax.fori_loop(0, 4, narrow, 0)


def layer(recv, slot_row, slot_col, w_proj, w_out, layer_grad):
    vm = pltpu.VMEM
    return pl.pallas_call(
        layer_kernel,
        out_shape=(
            jax.ShapeDtypeStruct((EVENTS, 512), BF),
            jax.ShapeDtypeStruct((OWNERS, 2, 16, 128), BF),
            jax.ShapeDtypeStruct((512, 2048), BF),
            jax.ShapeDtypeStruct((512, 512), BF),
        ),
        scratch_shapes=[
            vm((4096, 128), F32),
            vm((1024, 512), BF),
            vm((EVENTS, 512), F32),
            vm((EVENTS, 512), BF),
            vm((EVENTS, 512), F32),
            vm((EVENTS, 2048), F32),
            vm((EVENTS, 2048), BF),
            vm((EVENTS, 512), F32),
            vm((EVENTS, 512), F32),
            vm((EVENTS, 512), BF),
            vm((EVENTS, 2048), BF),
            vm((EVENTS, 512), BF),
            vm((EVENTS, 128), F32),
            vm((EVENTS, 128), F32),
            vm((EVENTS, 128), F32),
        ],
        compiler_params=pltpu.CompilerParams(vmem_limit_bytes=VMEM_LIMIT),
        name="layer",
    )(recv, slot_row, slot_col, w_proj, w_out, layer_grad)


def core_grad_kernel(
    arrived_ref, tile_ref, spread_ref, part_ref, lt_ref, middle_ref,
    first_out, middle_out, last_out,
    flipped, pg, ls, ss, fterm, lterm, first_acc, last_acc,
):
    half = pl.program_id(0)
    arrived = arrived_ref[...].reshape(OWNERS, 128)
    flipped[...] = jnp.transpose(arrived.astype(F32)).astype(I32) - 1
    _, middle_col, _ = index_columns(arrived, half)
    mask0, mask1 = slice_masks(middle_col)
    group = 16
    low = low_lanes((group, 8, 128))
    own = (iota((group, 16, 128), 1) // 8) == (iota((group, 16, 128), 2) // 64)

    def events(i, carry):
        srcs = pl.ds(pl.multiple_of(i * group, group), group)
        tile = tile_ref[srcs, 0]
        g = jnp.concatenate([tile[:, :, 0:64], tile[:, :, 64:128]], axis=1)
        wide = pl.ds(pl.multiple_of(i * group * 16, group * 16), group * 16)
        terms = bdot(g, part_ref[srcs], 2, 1)
        for side in range(2):
            x = terms[:, side * 16 : (side + 1) * 16, side * 128 : (side + 1) * 128]
            x = jnp.where(own, x, 0.0).reshape(group * 16, 128)
            ls[side, wide, :] = x + half_turn(x)
        grads = bdot(g, lt_ref[srcs], 1, 1)
        for pair in range(4):
            lanes = slice(pair * 128, (pair + 1) * 128)
            for side in range(2):
                even = grads[:, pair * 16 : pair * 16 + 8, side * 128 : (side + 1) * 128]
                odd = grads[:, pair * 16 + 8 : pair * 16 + 16, side * 128 : (side + 1) * 128]
                v0 = jnp.where(low, even, half_turn(odd))
                v1 = jnp.where(low, half_turn(even), odd)
                for t, v in ((2 * side, v0), (2 * side + 1, v1)):
                    at = pl.ds(pl.multiple_of(t * 1024 + i * group * 8, group * 8), group * 8)
                    pg[at, lanes] = v.reshape(group * 8, 128).astype(BF)
        return carry

    lax.fori_loop(0, OWNERS // group, events, 0)
    low = low_lanes((128, 128))
    middle_part = jnp.zeros((256, 512), F32)
    for t in range(4):
        at = slice(t * 1024, (t + 1) * 1024)
        middle_part += dot(spread_ref[at, :], pg[at, :], 0, 0)
        back = dot(pg[at, :], middle_ref[...], 1, 1)
        ss[0] = back[:, 0:128]
        ss[1] = back[:, 128:256]
        rows = slice(t * 128, (t + 1) * 128)
        m0, m1 = mask0[rows], mask1[rows]
        for pair in range(4):
            lanes = slice(pair * 128, (pair + 1) * 128)
            found = []
            for odd in range(2):
                where = pl.ds(pair * 2 + odd, 128, stride=8)
                x = jnp.where(m0, ss[0, where, :], 0.0) + jnp.where(m1, ss[1, where, :], 0.0)
                found.append(x + half_turn(x))
            fterm[rows, lanes] = jnp.where(low, found[0], found[1]).astype(BF)
            base = (t % 2) * 8 + pair * 2
            y0 = ls[t // 2, pl.ds(base, 128, stride=16), :]
            y1 = ls[t // 2, pl.ds(base + 1, 128, stride=16), :]
            lterm[rows, lanes] = jnp.where(low, y0, y1).astype(BF)

    source = iota((512, 512), 0)
    perm = one_hot(iota((512, 512), 1) == (source % 64) * 8 + source // 64)
    lterm[...] = dot(lterm[...], perm).astype(BF)

    def index_row(digit):
        return jnp.concatenate([flipped[pl.ds(digit * 8 + half * 4 + t, 1), :] for t in range(4)], axis=1)

    first_row = index_row(0)
    last_row = index_row(2)

    @pl.when(half == 0)
    def _():
        middle_out[...] = middle_part
        first_acc[...] = jnp.zeros_like(first_acc)
        last_acc[...] = jnp.zeros_like(last_acc)

    @pl.when(half == 1)
    def _():
        middle_out[...] += middle_part

    def scatter_first(i, carry):
        at = pl.ds(pl.multiple_of(i * 256, 256), 256)
        place = one_hot(iota((256, 512), 0) + i * 256 == first_row)
        first_acc[at, :] += dot(place, fterm[...])
        return carry

    def scatter_last(i, carry):
        at = pl.ds(pl.multiple_of(i * 256, 256), 256)
        place = one_hot(iota((256, 512), 0) + i * 256 == last_row)
        last_acc[at, :] += dot(place, lterm[...])
        return carry

    lax.fori_loop(0, 8, scatter_first, 0)
    lax.fori_loop(0, 4, scatter_last, 0)

    @pl.when(half == 1)
    def _():
        first_out[...] = first_acc[...].astype(BF)
        last_out[...] = last_acc[...].astype(BF)


def core_grads(arrived, tiles, spread, part, lt, middle_core):
    vm = pltpu.VMEM
    return pl.pallas_call(
        core_grad_kernel,
        grid=(2,),
        in_specs=[
            pl.BlockSpec((OWNERS, 1, 128), lambda h: (0, 0, 0)),
            pl.BlockSpec((OWNERS, 1, 16, 128), lambda h: (0, h, 0, 0)),
            pl.BlockSpec((4096, 256), lambda h: (h, 0)),
            pl.BlockSpec((OWNERS, 64, 256), lambda h: (h, 0, 0)),
            pl.BlockSpec((OWNERS, 32, 256), lambda h: (h, 0, 0)),
            pl.BlockSpec((256, 512), lambda h: (0, 0)),
        ],
        out_specs=(
            pl.BlockSpec((2048, 512), lambda h: (0, 0)),
            pl.BlockSpec((256, 512), lambda h: (0, 0)),
            pl.BlockSpec((1024, 512), lambda h: (0, 0)),
        ),
        out_shape=(
            jax.ShapeDtypeStruct((2048, 512), BF),
            jax.ShapeDtypeStruct((256, 512), F32),
            jax.ShapeDtypeStruct((1024, 512), BF),
        ),
        scratch_shapes=[
            vm((128, 128), I32),
            vm((4096, 512), BF),
            vm((2, 2048, 128), F32),
            vm((2, 1024, 128), F32),
            vm((512, 512), BF),
            vm((512, 512), BF),
            vm((2048, 512), F32),
            vm((1024, 512), F32),
        ],
        compiler_params=pltpu.CompilerParams(vmem_limit_bytes=VMEM_LIMIT),
        name="core_grads",
    )(arrived, tiles, spread, part, lt, middle_core)


def exchange(x):
    return lax.all_to_all(x, AXES, split_axis=0, concat_axis=0, tiled=True)


def per_device(item_digits, first_core, middle_core, last_core, w_proj, w_out, layer_grad):
    message, slot_row, slot_col = prep(item_digits)
    arrived = exchange(message)
    built, spread, part, lt = build(arrived, first_core, middle_core, last_core)
    recv = exchange(built)
    layer_rows, sent, proj_grad, out_grad = layer(recv, slot_row, slot_col, w_proj, w_out, layer_grad)
    tiles = exchange(sent)
    first_part, grad_middle, last_part = core_grads(arrived, tiles, spread, part, lt, middle_core)
    grad_first, grad_last, proj_total, out_total = lax.psum(
        tuple(x.astype(F32) for x in (first_part, last_part, proj_grad, out_grad)), AXES
    )
    return (layer_rows, grad_first, grad_middle, grad_last, proj_total, out_total)


def solution(mesh):
    return jax.shard_map(
        per_device,
        mesh=mesh,
        in_specs=(
            P(None, AXES),
            P(),
            P(AXES, None),
            P(),
            P(),
            P(),
            P(AXES, None),
        ),
        out_specs=(P(AXES, None), P(), P(AXES, None), P(), P(), P()),
        check_vma=False,
    )
```

time: 540 us -> 281 us (0.52)
  local copies, waits for them, and re-layouts: 184 us -> 0.97 us
  waiting for transfers between devices: 161 us -> 19.4 us
  blocking collectives: 22.9 us -> 163 us
  matrix products: 96.4 us -> 0 us
  Pallas kernels: 0 us -> 91.6 us
  other arithmetic: 44.7 us -> 0 us
  between operations: 14.6 us -> 0.65 us
  starting transfers between devices: 10.1 us -> 4.35 us
    psum x1 -> x0, waiting for transfers between devices: 130 us -> none  [per_device(): lax.psum((first_part, last_part, proj_grad.astype(jnp.float32), out_grad....]
    psum x0 -> x1, blocking collectives: none -> 117 us  [per_device(): lax.psum(tuple((x.astype(F32) for x in (first_part, last_part, proj_grad,...]
    dot_general x18 -> x0, matrix products: 96.4 us -> none  [the longest x1 14.6 us: per_device(): jnp.einsum('nabs,nabc->nsc', partial_four, row_four, preferred_element_ty...]
    pallas_call x0 -> x4, Pallas kernels: none -> 91.6 us  [the longest x1 33.1 us: layer(): pl.pallas_call(layer_kernel, out_shape=(jax.ShapeDtypeStruct((EVENTS, 512...]
    reshape x10 -> x0, local copies, waits for them, and re-layouts: 55.8 us -> none  [the longest x1 22.9 us: per_device(): grad_flat = partial_grad.reshape(count * D1, D2 * RANK)]
    convert_element_type x6 -> x0, local copies, waits for them, and re-layouts: 48 us -> none  [the longest x1 25.2 us: per_device(): built = jnp.einsum('nabs,nsc->nabc', partial_four, last_rows, preferred_e...]
    all_to_all x1 -> x2, blocking collectives: 22.9 us -> 46.1 us  [exchange(): return lax.all_to_all(x, AXES, split_axis=0, concat_axis=0, tiled=True)]
    another operation x4 -> x0, local copies, waits for them, and re-layouts: 22.3 us -> none  [the longest x1 22.3 us: per_device(): row_four = grad_arrived.reshape(count, D1, D2, D3)]
  transfers between devices with their start and end apart: 3 -> 1, of which waited for: 3 -> 1; matrix products, arithmetic and copies ran while one was open for 7% -> 0% of each run, Pallas kernels for 0% -> 0%
where the time goes in v1:
time: 281 us; the launch traced here: 280 us
  blocking collectives  163 us (58%)
  Pallas kernels  91.6 us (33%)
  waiting for transfers between devices  19.4 us (7%)
  starting transfers between devices  4.35 us (2%)
    psum x1, blocking collectives, per_device(): lax.psum(tuple((x.astype(F32) for x in (first_part, last_part, proj_grad,...  117 us
    all_to_all x2, blocking collectives, exchange(): return lax.all_to_all(x, AXES, split_axis=0, concat_axis=0, tiled=True)  46.1 us
    pallas_call x1, Pallas kernels, layer(): pl.pallas_call(layer_kernel, out_shape=(jax.ShapeDtypeStruct((EVENTS, 512...  33.1 us
    pallas_call x1, Pallas kernels, core_grads(): pl.pallas_call(core_grad_kernel, grid=(2,), in_specs=[pl.BlockSpec((OWNER...  30.5 us
    pallas_call x1, Pallas kernels, build(): pl.pallas_call(build_kernel, grid=(2,), in_specs=[pl.BlockSpec((OWNERS, 1...  25.6 us
    all_to_all x1, waiting for transfers between devices, exchange(): return lax.all_to_all(x, AXES, split_axis=0, concat_axis=0, tiled=True)  19.4 us
  transfers between devices with their start and end apart: 1, of which 1 were waited for; matrix products, arithmetic and copies ran while one was open for 0% of the time, Pallas kernels for 0%

profile of v1, /device:TPU:1, one launch (start us, length us, event | category | flops | bytes accessed | tf_op | source)
XLA Modules:
  0.0 280.5 jit_solution(7675414829809633579)
XLA Ops:
  0.6 2.3 prep.1
  3.0 21.3 %all_to_all.15.arrived_ref = s32[128,1,128]{2,1,0:T(1,128)} all-to-all(s32[128,1,128]{2,1,0:T(1,128)} %get-tuple-element.20), channel_id=1, replica_groups=mesh['dp'=16,'cores'=8] {'dp','cores'}, dimensions={0} | all-to-all | bytes 131072 | tf_op jit(solution)/shard_map/all_to_all | solution.py:547
  24.2 25.6 %build.1 = (bf16[128,2,16,128]{3,2,1,0:T(8,128)(2,1)}, bf16[8192,256]{1,0:T(8,128)(2,1)}, bf16[256,64,256]{2,1,0:T(8,128)(2,1)}, bf16[256,32,256]{2,1,0:T(8,128)(2,1)}) custom-call(s32[128,1,128]{2,1,0:T(1,128)} %all_to_all.15.arrived_ref, bf16[2048,512]{1,0:T(8,128)(2,1)} %first_ref.1, bf16[256,512]{1,0:T(8,128)(2,1)} %middle_ref.3, bf16[1024,512]{1,0:T(8,128)(2,1)} %last_ref.1), custom_call_target="tpu_custom_call" | custom-call | tf_op jit(solution)/shard_map/build/pallas_call | solution.py:172
  49.9 24.9 %all_to_all.16.recv_ref = bf16[128,2,16,128]{3,2,1,0:T(8,128)(2,1)} all-to-all(bf16[128,2,16,128]{3,2,1,0:T(8,128)(2,1)} %get-tuple-element.21), channel_id=1, replica_groups=mesh['dp'=16,'cores'=8] {'dp','cores'}, dimensions={0} | all-to-all | bytes 2097152 | tf_op jit(solution)/shard_map/all_to_all | solution.py:547
  74.7 33.1 %layer.1 = (bf16[512,512]{1,0:T(8,128)(2,1)}, bf16[128,2,16,128]{3,2,1,0:T(8,128)(2,1)}, bf16[512,2048]{1,0:T(8,128)(2,1)}, bf16[512,512]{1,0:T(8,128)(2,1)}) custom-call(bf16[128,2,16,128]{3,2,1,0:T(8,128)(2,1)} %all_to_all.16.recv_ref, s32[8,512]{1,0:T(8,128)} %get-tuple-element.22.slot_row_ref, s32[512,128]{1,0:T(8,128)} %get-tuple-element.23.slot_col_ref, ...), custom_call_target="tpu_custom_call" | custom-call | tf_op jit(solution)/shard_map/layer/pallas_call | solution.py:376
  107.8 4.3 %all-to-all-start.2 = ((bf16[128,2,16,128]{3,2,1,0:T(8,128)(2,1)}), bf16[128,2,16,128]{3,2,1,0:T(8,128)(2,1)S(1)}, u32[]{:S(2)}, u32[]{:S(2)}) async-start(bf16[128,2,16,128]{3,2,1,0:T(8,128)(2,1)} %get-tuple-element.25), calls=%async_computation.2 | async-start | bytes 2097152 | tf_op jit(solution)/shard_map/all_to_all | solution.py:547
  112.2 19.4 %all-to-all-done.2.tile_ref = bf16[128,2,16,128]{3,2,1,0:T(8,128)(2,1)S(1)} async-done(((bf16[128,2,16,128]{3,2,1,0:T(8,128)(2,1)}), bf16[128,2,16,128]{3,2,1,0:T(8,128)(2,1)S(1)}, u32[]{:S(2)}, u32[]{:S(2)}) %all-to-all-start.2) | async-done | bytes 1048608 | tf_op jit(solution)/shard_map/all_to_all | solution.py:547
  131.6 0.0 copy-start
  131.6 1.0 copy-done
  132.6 0.0 copy-start.1
  132.6 30.5 %core_grads.1 = (bf16[2048,512]{1,0:T(8,128)(2,1)}, f32[256,512]{1,0:T(8,128)}, bf16[1024,512]{1,0:T(8,128)(2,1)}) custom-call(s32[128,1,128]{2,1,0:T(1,128)} %all_to_all.15.arrived_ref, bf16[128,2,16,128]{3,2,1,0:T(8,128)(2,1)} %copy-done, bf16[8192,256]{1,0:T(8,128)(2,1)} %get-tuple-element.26.spread_ref, ...), custom_call_target="tpu_custom_call" | custom-call | tf_op jit(solution)/shard_map/core_grads/pallas_call | solution.py:510
  163.1 0.0 copy-done.1
  163.1 117.4 %all-reduce.2 = (f32[2048,512]{1,0:T(8,128)}, f32[1024,512]{1,0:T(8,128)}, f32[512,2048]{1,0:T(8,128)}, f32[512,512]{1,0:T(8,128)}) all-reduce(bf16[2048,512]{1,0:T(8,128)(2,1)} %get-tuple-element.29, bf16[1024,512]{1,0:T(8,128)(2,1)} %get-tuple-element.31, ...), channel_id=1, replica_groups=mesh['dp'=16,'cores'=8] {'dp','cores'}, use_global_device_ids=true, to_apply=%region_0.0 | all-reduce | flops 2883584 | bytes 17301504 | tf_op jit(solution)/shard_map/psum | solution.py:558
Async XLA Ops:
  107.8 23.8 %all-to-all-start.2 = ((bf16[128,2,16,128]{3,2,1,0:T(8,128)(2,1)}), bf16[128,2,16,128]{3,2,1,0:T(8,128)(2,1)S(1)}, u32[]{:S(2)}, u32[]{:S(2)}) async-start(bf16[128,2,16,128]{3,2,1,0:T(8,128)(2,1)} %get-tuple-element.25), calls=%async_computation.2 | async-start | bytes 2097152 | tf_op jit(solution)/shard_map/all_to_all | solution.py:547
  131.6 1.0 copy-start
  132.6 30.5 %copy-start.1 = (bf16[512,2048]{1,0:T(8,128)(2,1)S(1)}, bf16[512,2048]{1,0:T(8,128)(2,1)}, u32[]{:S(2)}) copy-start(bf16[512,2048]{1,0:T(8,128)(2,1)} %get-tuple-element.32) | copy-start | bytes 6291460

commit v2 on v1

--- a/solution.py
+++ b/solution.py
@@ -15,6 +15,7 @@
 EVENTS = 512
 OWNERS = 128
 VMEM_LIMIT = 56 * 1024 * 1024
+MESH = pl.DeviceIdType.MESH
 
 
 def iota(shape, dim):
@@ -41,7 +42,14 @@
     return jnp.where(flag, 1.0, 0.0).astype(BF)
 
 
-def prep_kernel(dig_ref, msg_ref, slot_row_ref, slot_col_ref):
+def prep_kernel(dig_ref, arrived_ref, slot_row_ref, slot_col_ref, message, stage, send_sem, recv_sem):
+    dp = lax.axis_index("dp")
+    cores = lax.axis_index("cores")
+    barrier = pltpu.get_barrier_semaphore()
+    row_mates = [(lax.rem(cores + i, 8), (dp, lax.rem(cores + i, 8))) for i in range(1, 8)]
+    column_mates = [(lax.rem(dp + i, 16), (lax.rem(dp + i, 16), cores)) for i in range(1, 16)]
+    for _, who in row_mates + column_mates:
+        pl.semaphore_signal(barrier, inc=1, device_id=who, device_id_type=MESH)
     digits = dig_ref[...]
     padded = jnp.concatenate([digits, jnp.zeros((5, EVENTS), I32)], axis=0).astype(F32)
     cols = jnp.transpose(padded).astype(I32)
@@ -60,21 +68,56 @@
     part = jnp.where(place < 32, value >> 4, value & 15)
     ok = (inner % 8 == rank_col) & (inner < 24) & (place < 64)
     table = jnp.where(ok, part, 0).astype(F32).astype(BF)
-    pick = one_hot(iota((OWNERS, EVENTS), 0) == owner_row)
+    pick = one_hot(iota((OWNERS, EVENTS), 0) == (owner_row & 7) * 16 + (owner_row >> 3))
     sums = dot(pick, table)
     whole = sums * 16.0 + pltpu.roll(sums, 96, 1)
-    msg_ref[...] = jnp.where(iota((OWNERS, 128), 1) < 24, whole, 0.0).astype(I32).reshape(OWNERS, 1, 128)
+    whole = jnp.where(iota((OWNERS, 128), 1) < 24, whole, 0.0).astype(I32)
+    message[...] = whole.reshape(8, 16, 1, 128)
+    pl.semaphore_wait(barrier, 22)
+
+    def start(number, src, dst, who):
+        copy = pltpu.make_async_remote_copy(
+            src_ref=src,
+            dst_ref=dst,
+            send_sem=send_sem.at[number],
+            recv_sem=recv_sem.at[number],
+            device_id=who,
+            device_id_type=MESH,
+        )
+        copy.start()
+        return copy
+
+    first = [start(n, message.at[c], stage.at[cores], who) for n, (c, who) in enumerate(row_mates)]
+    stage[cores] = message[cores]
+    for copy in first:
+        copy.wait_recv()
+    second = [
+        start(7 + n, stage.at[:, d], arrived_ref.at[dp], who) for n, (d, who) in enumerate(column_mates)
+    ]
+    arrived_ref[dp] = stage[:, dp]
+    for copy in second:
+        copy.wait_recv()
+    for copy in first + second:
+        copy.wait_send()
 
 
 def prep(digits):
     return pl.pallas_call(
         prep_kernel,
         out_shape=(
-            jax.ShapeDtypeStruct((OWNERS, 1, 128), I32),
+            jax.ShapeDtypeStruct((16, 8, 1, 128), I32),
             jax.ShapeDtypeStruct((8, EVENTS), I32),
             jax.ShapeDtypeStruct((EVENTS, 128), I32),
         ),
-        compiler_params=pltpu.CompilerParams(vmem_limit_bytes=VMEM_LIMIT),
+        scratch_shapes=[
+            pltpu.VMEM((8, 16, 1, 128), I32),
+            pltpu.VMEM((8, 16, 1, 128), I32),
+            pltpu.SemaphoreType.DMA((22,)),
+            pltpu.SemaphoreType.DMA((22,)),
+        ],
+        compiler_params=pltpu.CompilerParams(
+            collective_id=1, has_side_effects=True, vmem_limit_bytes=VMEM_LIMIT
+        ),
         name="prep",
     )(digits)
 
@@ -336,7 +379,7 @@
 
     for block in range(4):
         lanes = slice(block * 512, (block + 1) * 512)
-        dproj_ref[:, lanes] = dot(normed[...], dz[:, lanes], 0, 0).astype(BF)
+        dproj_ref[lanes, :] = dot(normed[...], dz[:, lanes], 0, 0).astype(BF)
 
     back = one_hot(source == (target % 8) * 64 + ((target // 8) % 8) * 8 + target // 64)
 
@@ -378,7 +421,7 @@
         out_shape=(
             jax.ShapeDtypeStruct((EVENTS, 512), BF),
             jax.ShapeDtypeStruct((OWNERS, 2, 16, 128), BF),
-            jax.ShapeDtypeStruct((512, 2048), BF),
+            jax.ShapeDtypeStruct((2048, 512), BF),
             jax.ShapeDtypeStruct((512, 512), BF),
         ),
         scratch_shapes=[
@@ -543,21 +586,222 @@
     )(arrived, tiles, spread, part, lt, middle_core)
 
 
+class Place:
+    def __init__(self):
+        dp = lax.axis_index("dp")
+        cores = lax.axis_index("cores")
+        self.at = (cores // 2, dp // 4, lax.rem(dp, 4))
+        self.core = lax.rem(cores, 2)
+
+    def along(self, dim, offset):
+        at = list(self.at)
+        at[dim] = lax.rem(at[dim] + offset, 4)
+        return at[dim], (at[1] * 4 + at[2], at[0] * 2 + self.core)
+
+    def sibling(self):
+        x, y, z = self.at
+        return (y * 4 + z, x * 2 + 1 - self.core)
+
+
+ORDERS = ((0, 1, 2), (1, 2, 0), (2, 0, 1))
+SIZES = (256, 64, 16)
+
+
+def reduce_kernel(
+    first_ref, proj_ref, last_ref, out_ref,
+    total0, total1, total2,
+    rest, pair0, pair1, pair2, sum0, sum1, sum2,
+    got00, got01, got02, got10, got11, got12, got20, got21, got22, send_sem, recv_sem,
+):
+    place = Place()
+    core = place.core
+    barrier = pltpu.get_barrier_semaphore()
+    partners = [place.sibling()] + [place.along(d, o)[1] for d in range(3) for o in (1, 2, 3)]
+    for who in partners:
+        pl.semaphore_signal(barrier, inc=1, device_id=who, device_id_type=MESH)
+    for block in range(12):
+        row = (block // 3) * 512
+        lanes = slice((block % 3) * 128, (block % 3 + 1) * 128)
+        if block < 8:
+            value = last_ref[(block // 4) * 512 : (block // 4 + 1) * 512, (block % 4) * 128 : (block % 4 + 1) * 128]
+        else:
+            value = out_ref[:, (block % 4) * 128 : (block % 4 + 1) * 128]
+        rest[row : row + 512, lanes] = value
+    source = (first_ref, proj_ref, rest)
+    total = (total0, total1, total2)
+    pair = (pair0, pair1, pair2)
+    sums = (sum0, sum1, sum2)
+    got = ((got00, got01, got02), (got10, got11, got12), (got20, got21, got22))
+    pl.semaphore_wait(barrier, len(partners))
+    pending = []
+
+    def start(part, stage, slot, src, dst, who):
+        copy = pltpu.make_async_remote_copy(
+            src_ref=src,
+            dst_ref=dst,
+            send_sem=send_sem.at[part, stage, slot],
+            recv_sem=recv_sem.at[part, stage, slot],
+            device_id=who,
+            device_id_type=MESH,
+        )
+        copy.start()
+        pending.append(copy)
+        return copy
+
+    def rows(start_row, size):
+        return pl.ds(pl.multiple_of(start_row, 16), size)
+
+    base = [core * 1024 for _ in range(3)]
+    flight = {}
+    for slot in (1, 2, 3, 0):
+        for part in range(3):
+            quarter, _ = place.along(ORDERS[part][0], slot)
+            flight[part, slot] = start(
+                part, 0, slot,
+                source[part].at[rows((1 - core) * 1024 + quarter * 256, 256)],
+                pair[part].at[rows(quarter * 256, 256)],
+                place.sibling(),
+            )
+    moving = {}
+    for slot in (1, 2, 3, 0):
+        for part in range(3):
+            quarter, who = place.along(ORDERS[part][0], slot)
+            flight[part, slot].wait_recv()
+            at = rows(quarter * 256, 256)
+            mine = source[part][rows(core * 1024 + quarter * 256, 256), :].astype(F32)
+            sums[part][at, :] = (mine + pair[part][at, :].astype(F32)).astype(BF)
+            if slot:
+                moving[part, slot] = start(part, 1, slot, sums[part].at[at], got[part][0].at[slot - 1], who)
+    offset = [0, 0, 0]
+    for level in range(3):
+        size = SIZES[level]
+        following = {}
+        for part in range(3):
+            mine = place.at[ORDERS[part][level]]
+            offset[part] = offset[part] + mine * size
+            for slot in (1, 2, 3):
+                moving[part, slot].wait_recv()
+            at = rows(offset[part], size)
+            value = sums[part][at, :].astype(F32)
+            for slot in range(3):
+                value = value + got[part][level][slot].astype(F32)
+            if level < 2:
+                sums[part][at, :] = value.astype(BF)
+                for slot in (1, 2, 3):
+                    quarter, who = place.along(ORDERS[part][level + 1], slot)
+                    src = sums[part].at[rows(offset[part] + quarter * SIZES[level + 1], SIZES[level + 1])]
+                    following[part, slot] = start(part, level + 2, slot, src, got[part][level + 1].at[slot - 1], who)
+            else:
+                where = rows(core * 1024 + offset[part], size)
+                total[part][where, :] = value.astype(BF)
+                for slot in (1, 2, 3):
+                    who = place.along(ORDERS[part][2], slot)[1]
+                    ref = total[part].at[where]
+                    following[part, slot] = start(part, 4, slot, ref, ref, who)
+        moving = following
+    final = []
+    for level in (1, 0):
+        following = {}
+        for part in range(3):
+            mine = place.at[ORDERS[part][level + 1]]
+            offset[part] = offset[part] - mine * SIZES[level + 1]
+            for slot in (1, 2, 3):
+                moving[part, slot].wait_recv()
+            where = rows(core * 1024 + offset[part], SIZES[level])
+            ref = total[part].at[where]
+            for slot in (1, 2, 3):
+                who = place.along(ORDERS[part][level], slot)[1]
+                following[part, slot] = start(part, 6 - level, slot - 0, ref, ref, who)
+            if level == 0:
+                final.append(start(part, 7, 0, ref, ref, place.sibling()))
+        moving = following
+    for slot in (1, 3, 2):
+        for part in range(3):
+            moving[part, slot].wait_recv()
+            quarter = place.along(ORDERS[part][0], 4 - slot)[0]
+            ref = total[part].at[rows(core * 1024 + quarter * 256, 256)]
+            final.append(start(part, 7, slot, ref, ref, place.sibling()))
+    for copy in final:
+        copy.wait_recv()
+    for copy in pending:
+        copy.wait_send()
+
+
+def reduce_all(first_part, proj_grad, last_part, out_grad, ident):
+    vm = pltpu.VMEM
+    widths = (512, 512, 384)
+    return pl.pallas_call(
+        reduce_kernel,
+        out_shape=tuple(jax.ShapeDtypeStruct((2048, w), BF) for w in widths),
+        in_specs=[pl.BlockSpec(memory_space=vm)] * 4,
+        out_specs=tuple(pl.BlockSpec(memory_space=vm) for _ in widths),
+        scratch_shapes=[vm((2048, 384), BF)]
+        + [vm((1024, w), BF) for w in widths]
+        + [vm((1024, w), BF) for w in widths]
+        + [vm((3, size, w), BF) for w in widths for size in SIZES]
+        + [pltpu.SemaphoreType.DMA((3, 8, 4))] * 2,
+        compiler_params=pltpu.CompilerParams(
+            collective_id=ident, has_side_effects=True, vmem_limit_bytes=VMEM_LIMIT
+        ),
+        name="reduce_all",
+    )(first_part, proj_grad, last_part, out_grad)
+
+
+def widen_kernel(a_ref, b_ref, c_ref, first_ref, last_ref, proj_ref, out_ref):
+    step = pl.program_id(0)
+    first_ref[...] = a_ref[...].astype(F32)
+    proj_ref[...] = b_ref[...].astype(F32)
+    block0 = step * 3
+    for k in range(3):
+        block = block0 + k
+        value = c_ref[:, k * 128 : (k + 1) * 128].astype(F32)
+        for lane in range(4):
+
+            @pl.when((block < 8) & (block % 4 == lane))
+            def _():
+                last_ref[pl.ds(pl.multiple_of((block // 4) * 512, 512), 512), lane * 128 : (lane + 1) * 128] = value
+
+            @pl.when((block >= 8) & (block % 4 == lane))
+            def _():
+                out_ref[:, lane * 128 : (lane + 1) * 128] = value
+
+
+def widen(a, b, c):
+    return pl.pallas_call(
+        widen_kernel,
+        grid=(4,),
+        in_specs=[pl.BlockSpec((512, w), lambda i: (i, 0)) for w in (512, 512, 384)],
+        out_specs=(
+            pl.BlockSpec((512, 512), lambda i: (i, 0)),
+            pl.BlockSpec((1024, 512), lambda i: (0, 0)),
+            pl.BlockSpec((512, 512), lambda i: (0, i)),
+            pl.BlockSpec((512, 512), lambda i: (0, 0)),
+        ),
+        out_shape=(
+            jax.ShapeDtypeStruct((2048, 512), F32),
+            jax.ShapeDtypeStruct((1024, 512), F32),
+            jax.ShapeDtypeStruct((512, 2048), F32),
+            jax.ShapeDtypeStruct((512, 512), F32),
+        ),
+        compiler_params=pltpu.CompilerParams(vmem_limit_bytes=VMEM_LIMIT),
+        name="widen",
+    )(a, b, c)
+
+
 def exchange(x):
     return lax.all_to_all(x, AXES, split_axis=0, concat_axis=0, tiled=True)
 
 
 def per_device(item_digits, first_core, middle_core, last_core, w_proj, w_out, layer_grad):
-    message, slot_row, slot_col = prep(item_digits)
-    arrived = exchange(message)
+    arrived, slot_row, slot_col = prep(item_digits)
+    arrived = arrived.reshape(OWNERS, 1, 128)
     built, spread, part, lt = build(arrived, first_core, middle_core, last_core)
     recv = exchange(built)
     layer_rows, sent, proj_grad, out_grad = layer(recv, slot_row, slot_col, w_proj, w_out, layer_grad)
     tiles = exchange(sent)
     first_part, grad_middle, last_part = core_grads(arrived, tiles, spread, part, lt, middle_core)
-    grad_first, grad_last, proj_total, out_total = lax.psum(
-        tuple(x.astype(F32) for x in (first_part, last_part, proj_grad, out_grad)), AXES
-    )
+    totals = reduce_all(first_part, proj_grad, last_part, out_grad, 2)
+    grad_first, grad_last, proj_total, out_total = widen(*totals)
     return (layer_rows, grad_first, grad_middle, grad_last, proj_total, out_total)
 
 

time: 281 us -> 224 us (0.80)
  blocking collectives: 163 us -> 50.8 us
  Pallas kernels: 91.6 us -> 172 us
  waiting for transfers between devices: 19.4 us -> 0 us
  starting transfers between devices: 4.35 us -> 0 us
    psum x1 -> x0, blocking collectives: 117 us -> none  [per_device(): lax.psum(tuple((x.astype(F32) for x in (first_part, last_part, proj_grad,...]
    pallas_call x1 -> x3, Pallas kernels: 2.34 us -> 82.9 us  [the longest x1 57.5 us: reduce_all(): pl.pallas_call(reduce_kernel, out_shape=tuple((jax.ShapeDtypeStruct((2048...]
    all_to_all x1 -> x0, waiting for transfers between devices: 19.4 us -> none  [exchange(): return lax.all_to_all(x, AXES, split_axis=0, concat_axis=0, tiled=True)]
    all_to_all x2, blocking collectives: 46.1 us -> 50.8 us  [exchange(): return lax.all_to_all(x, AXES, split_axis=0, concat_axis=0, tiled=True)]
    all_to_all x1 -> x0, starting transfers between devices: 4.35 us -> none  [exchange(): return lax.all_to_all(x, AXES, split_axis=0, concat_axis=0, tiled=True)]
  transfers between devices with their start and end apart: 1 -> 0, of which waited for: 1 -> 0; matrix products, arithmetic and copies ran while one was open for 0% -> 0% of each run, Pallas kernels for 0% -> 0%
where the time goes in v2:
time: 224 us
  Pallas kernels  172 us (77%)
  blocking collectives  50.8 us (23%)
    pallas_call x1, Pallas kernels, reduce_all(): pl.pallas_call(reduce_kernel, out_shape=tuple((jax.ShapeDtypeStruct((2048...  57.5 us
    all_to_all x2, blocking collectives, exchange(): return lax.all_to_all(x, AXES, split_axis=0, concat_axis=0, tiled=True)  50.8 us
    pallas_call x1, Pallas kernels, layer(): pl.pallas_call(layer_kernel, out_shape=(jax.ShapeDtypeStruct((EVENTS, 512...  33.1 us
    pallas_call x1, Pallas kernels, core_grads(): pl.pallas_call(core_grad_kernel, grid=(2,), in_specs=[pl.BlockSpec((OWNER...  30.4 us
    pallas_call x1, Pallas kernels, build(): pl.pallas_call(build_kernel, grid=(2,), in_specs=[pl.BlockSpec((OWNERS, 1...  25.6 us
    pallas_call x1, Pallas kernels, prep(): pl.pallas_call(prep_kernel, out_shape=(jax.ShapeDtypeStruct((16, 8, 1, 12...  17.6 us
    pallas_call x1, Pallas kernels, widen(): pl.pallas_call(widen_kernel, grid=(4,), in_specs=[pl.BlockSpec((512, w),...  7.71 us

profile of v2, /device:TPU:1, one launch (start us, length us, event | category | flops | bytes accessed | tf_op | source)
XLA Modules:
  0.0 223.7 jit_solution(6081292433100883904)
XLA Ops:
  0.6 17.6 %prep.1 = (s32[16,8,1,128]{3,2,1,0:T(1,128)}, s32[8,512]{1,0:T(8,128)}, s32[512,128]{1,0:T(8,128)}) custom-call(s32[3,512]{1,0:T(4,128)} %dig_ref.1), custom_call_target="tpu_custom_call" | custom-call | tf_op jit(solution)/shard_map/prep/pallas_call | solution.py:105
  18.3 25.6 %build.1 = (bf16[128,2,16,128]{3,2,1,0:T(8,128)(2,1)}, bf16[8192,256]{1,0:T(8,128)(2,1)}, bf16[256,64,256]{2,1,0:T(8,128)(2,1)}, bf16[256,32,256]{2,1,0:T(8,128)(2,1)}) custom-call(s32[128,1,128]{2,1,0:T(1,128)} %bitcast.1, bf16[2048,512]{1,0:T(8,128)(2,1)} %first_ref.1, bf16[256,512]{1,0:T(8,128)(2,1)} %middle_ref.3, bf16[1024,512]{1,0:T(8,128)(2,1)} %last_ref.1), custom_call_target="tpu_custom_call" | custom-call | tf_op jit(solution)/shard_map/build/pallas_call | solution.py:215
  43.9 26.1 %all_to_all.10.recv_ref = bf16[128,2,16,128]{3,2,1,0:T(8,128)(2,1)} all-to-all(bf16[128,2,16,128]{3,2,1,0:T(8,128)(2,1)} %get-tuple-element.28), channel_id=1, replica_groups=mesh['dp'=16,'cores'=8] {'dp','cores'}, dimensions={0} | all-to-all | bytes 2097152 | tf_op jit(solution)/shard_map/all_to_all | solution.py:792
  70.0 33.1 %layer.1 = (bf16[512,512]{1,0:T(8,128)(2,1)}, bf16[128,2,16,128]{3,2,1,0:T(8,128)(2,1)}, bf16[2048,512]{1,0:T(8,128)(2,1)}, bf16[512,512]{1,0:T(8,128)(2,1)}) custom-call(bf16[128,2,16,128]{3,2,1,0:T(8,128)(2,1)} %all_to_all.10.recv_ref, s32[8,512]{1,0:T(8,128)} %get-tuple-element.29.slot_row_ref, s32[512,128]{1,0:T(8,128)} %get-tuple-element.30.slot_col_ref, ...), custom_call_target="tpu_custom_call" | custom-call | tf_op jit(solution)/shard_map/layer/pallas_call | solution.py:419
  103.1 24.7 %all_to_all.11.tile_ref = bf16[128,2,16,128]{3,2,1,0:T(8,128)(2,1)} all-to-all(bf16[128,2,16,128]{3,2,1,0:T(8,128)(2,1)} %get-tuple-element.32), channel_id=1, replica_groups=mesh['dp'=16,'cores'=8] {'dp','cores'}, dimensions={0} | all-to-all | bytes 2097152 | tf_op jit(solution)/shard_map/all_to_all | solution.py:792
  127.8 30.4 %core_grads.1 = (bf16[2048,512]{1,0:T(8,128)(2,1)}, f32[256,512]{1,0:T(8,128)}, bf16[1024,512]{1,0:T(8,128)(2,1)}) custom-call(s32[128,1,128]{2,1,0:T(1,128)} %bitcast.2, bf16[128,2,16,128]{3,2,1,0:T(8,128)(2,1)} %all_to_all.11.tile_ref, bf16[8192,256]{1,0:T(8,128)(2,1)} %get-tuple-element.33.spread_ref, bf16[256,64,256]{2,1,0:T(8,128)(2,1)} %get-tuple-element.34.part_ref, ...), custom_call_target="tpu_custom_call" | custom-call | tf_op jit(solution)/shard_map/core_grads/pallas_call | solution.py:553
  158.2 57.5 %reduce_all.1 = (bf16[2048,512]{1,0:T(8,128)(2,1)}, bf16[2048,512]{1,0:T(8,128)(2,1)}, bf16[2048,384]{1,0:T(8,128)(2,1)}) custom-call(bf16[2048,512]{1,0:T(8,128)(2,1)} %get-tuple-element.36.first_ref, bf16[2048,512]{1,0:T(8,128)(2,1)} %get-tuple-element.37.proj_ref, bf16[1024,512]{1,0:T(8,128)(2,1)} %get-tuple-element.38.last_ref, ...), custom_call_target="tpu_custom_call" | custom-call | tf_op jit(solution)/shard_map/reduce_all/pallas_call | solution.py:733
  215.8 7.7 %widen.1 = (f32[2048,512]{1,0:T(8,128)}, f32[1024,512]{1,0:T(8,128)}, f32[512,2048]{1,0:T(8,128)}, f32[512,512]{1,0:T(8,128)}) custom-call(bf16[2048,512]{1,0:T(8,128)(2,1)} %get-tuple-element.40.a_ref, bf16[2048,512]{1,0:T(8,128)(2,1)} %get-tuple-element.41.b_ref, bf16[2048,384]{1,0:T(8,128)(2,1)} %get-tuple-element.42.c_ref), custom_call_target="tpu_custom_call" | custom-call | tf_op jit(solution)/shard_map/widen/pallas_call | solution.py:770

commit v3 on v2

--- a/solution.py
+++ b/solution.py
@@ -244,7 +244,7 @@
 
 
 def sigmoid(x):
-    return 1.0 / (1.0 + jnp.exp(-x))
+    return 0.5 * jnp.tanh(0.5 * x) + 0.5
 
 
 def norm_stats(x):
@@ -261,7 +261,7 @@
 def layer_kernel(
     recv_ref, slot_row_ref, slot_col_ref, proj_ref, out_ref, grad_ref,
     rows_ref, sent_ref, dproj_ref, dout_ref,
-    tiles, slots, emb, normed, y_in, z, act, mixed, y_mid, gated, dz, dmixed, work, sc_in, sc_mid,
+    tiles, slots, emb, normed, y_in, z, act, mixed, y_mid, gated, dz, dmixed, work, work_v, work_k, sc_in,
 ):
     low = low_lanes((256 // 2, 128))
     step = 128
@@ -305,25 +305,25 @@
     lax.fori_loop(0, EVENTS // step, project, 0)
     scaling = 1.0 / math.sqrt(128.0)
 
-    def scores_of(head, rows, base):
-        q = act[rows, pl.ds(pl.multiple_of(1024 + head * 128, 128), 128)]
-        k = act[:, pl.ds(pl.multiple_of(1536 + head * 128, 128), 128)]
+    def scores_of(head, block):
+        end = (block + 1) * step
+        q = act[block * step : end, pl.ds(pl.multiple_of(1024 + head * 128, 128), 128)]
+        k = act[0:end, pl.ds(pl.multiple_of(1536 + head * 128, 128), 128)]
         s = dot(q, k, 1, 1) * scaling
-        causal = base + iota((step, EVENTS), 0) >= iota((step, EVENTS), 1)
+        causal = block * step + iota((step, end), 0) >= iota((step, end), 1)
         return s, causal
 
-    def attend(j, carry):
-        head = j // 4
-        base = pl.multiple_of((j % 4) * step, step)
-        rows = pl.ds(base, step)
+    def attend(head, carry):
         cols = pl.ds(pl.multiple_of(head * 128, 128), 128)
-        s, causal = scores_of(head, rows, base)
-        weights = jnp.where(causal, s * sigmoid(s), 0.0).astype(BF)
-        v = act[:, pl.ds(pl.multiple_of(512 + head * 128, 128), 128)]
-        mixed[rows, cols] = dot(weights, v)
-        return carry
-
-    lax.fori_loop(0, 16, attend, 0)
+        for block in range(4):
+            end = (block + 1) * step
+            s, causal = scores_of(head, block)
+            weights = jnp.where(causal, s * sigmoid(s), 0.0).astype(BF)
+            v = act[0:end, pl.ds(pl.multiple_of(512 + head * 128, 128), 128)]
+            mixed[block * step : end, cols] = dot(weights, v)
+        return carry
+
+    lax.fori_loop(0, 4, attend, 0)
 
     def finish(i, carry):
         at = pl.ds(pl.multiple_of(i * step, step), step)
@@ -349,21 +349,24 @@
         vcols = pl.ds(pl.multiple_of(512 + head * 128, 128), 128)
         qcols = pl.ds(pl.multiple_of(1024 + head * 128, 128), 128)
         kcols = pl.ds(pl.multiple_of(1536 + head * 128, 128), 128)
-        d_v = jnp.zeros((EVENTS, 128), F32)
-        d_k = jnp.zeros((EVENTS, 128), F32)
-        for block in range(4):
-            base = block * step
-            rows = slice(base, base + step)
-            s, causal = scores_of(head, rows, base)
+        for block in (3, 2, 1, 0):
+            end = (block + 1) * step
+            rows = slice(block * step, end)
+            s, causal = scores_of(head, block)
             sig = sigmoid(s)
             weights = jnp.where(causal, s * sig, 0.0).astype(BF)
             dm = dmixed[rows, cols]
-            d_w = dot(dm, act[:, vcols], 1, 1).astype(BF).astype(F32)
+            d_w = dot(dm, act[0:end, vcols], 1, 1).astype(BF).astype(F32)
             d_s = jnp.where(causal, d_w * (sig * (1.0 + s * (1.0 - sig))) * scaling, 0.0).astype(BF)
-            d_v += dot(weights, dm, 0, 0)
-            d_k += dot(d_s, act[rows, qcols], 0, 0)
-            d_q = dot(d_s, act[:, kcols])
-            work[rows, :] = d_q
+            v_part = dot(weights, dm, 0, 0)
+            k_part = dot(d_s, act[rows, qcols], 0, 0)
+            if block == 3:
+                work_v[...] = v_part
+                work_k[...] = k_part
+            else:
+                work_v[0:end, :] += v_part
+                work_k[0:end, :] += k_part
+            work[rows, :] = dot(d_s, act[0:end, kcols])
 
         def through(ct, where):
             value = z[:, where]
@@ -371,8 +374,8 @@
             dz[:, where] = (ct.astype(BF).astype(F32) * (sig * (1.0 + value * (1.0 - sig)))).astype(BF)
 
         through(work[...], qcols)
-        through(d_v, vcols)
-        through(d_k, kcols)
+        through(work_v[...], vcols)
+        through(work_k[...], kcols)
         return carry
 
     lax.fori_loop(0, 4, attend_grad, 0)
@@ -437,6 +440,7 @@
             vm((EVENTS, 512), BF),
             vm((EVENTS, 2048), BF),
             vm((EVENTS, 512), BF),
+            vm((EVENTS, 128), F32),
             vm((EVENTS, 128), F32),
             vm((EVENTS, 128), F32),
             vm((EVENTS, 128), F32),
@@ -608,31 +612,58 @@
 
 
 def reduce_kernel(
-    first_ref, proj_ref, last_ref, out_ref,
-    total0, total1, total2,
-    rest, pair0, pair1, pair2, sum0, sum1, sum2,
-    got00, got01, got02, got10, got11, got12, got20, got21, got22, send_sem, recv_sem,
+    with_rows, *refs,
 ):
+    if with_rows:
+        rows_ref, refs = refs[0], refs[1:]
+    wide_ref, extra_ref = refs[:2]
+    refs = refs[2:]
+    if with_rows:
+        landed_ref, refs = refs[0], refs[1:]
+    total0, total1, total2, rest, pair0, pair1, pair2, sum0, sum1, sum2 = refs[:10]
+    got00, got01, got02, got10, got11, got12, got20, got21, got22 = refs[10:19]
+    halves0, halves1, halves2, send_sem, recv_sem = refs[19:24]
     place = Place()
     core = place.core
     barrier = pltpu.get_barrier_semaphore()
-    partners = [place.sibling()] + [place.along(d, o)[1] for d in range(3) for o in (1, 2, 3)]
-    for who in partners:
-        pl.semaphore_signal(barrier, inc=1, device_id=who, device_id_type=MESH)
-    for block in range(12):
-        row = (block // 3) * 512
-        lanes = slice((block % 3) * 128, (block % 3 + 1) * 128)
-        if block < 8:
-            value = last_ref[(block // 4) * 512 : (block // 4 + 1) * 512, (block % 4) * 128 : (block % 4 + 1) * 128]
+    if with_rows:
+        row_send, row_recv, own_sem = refs[24:]
+        me = lax.axis_index("dp") * 8 + lax.axis_index("cores")
+
+        def partner(i):
+            other = lax.rem(me + i, OWNERS)
+            return other, (other // 8, lax.rem(other, 8))
+
+        def greet(i, carry):
+            pl.semaphore_signal(barrier, inc=1, device_id=partner(i)[1], device_id_type=MESH)
+            return carry
+
+        lax.fori_loop(1, OWNERS, greet, 0)
+        expected = OWNERS - 1
+    else:
+        partners = [place.sibling()] + [place.along(d, o)[1] for d in range(3) for o in (1, 2, 3)]
+        for who in partners:
+            pl.semaphore_signal(barrier, inc=1, device_id=who, device_id_type=MESH)
+        expected = len(partners)
+    width = rest.shape[1]
+    for block in range(4):
+        if with_rows:
+            value = extra_ref[:, block * 128 : (block + 1) * 128]
         else:
-            value = out_ref[:, (block % 4) * 128 : (block % 4 + 1) * 128]
-        rest[row : row + 512, lanes] = value
-    source = (first_ref, proj_ref, rest)
+            value = extra_ref[(block // 2) * 512 : (block // 2 + 1) * 512, (block % 2) * 256 : (block % 2 + 1) * 256]
+        rest[block * 512 : (block + 1) * 512, :] = value
     total = (total0, total1, total2)
     pair = (pair0, pair1, pair2)
     sums = (sum0, sum1, sum2)
     got = ((got00, got01, got02), (got10, got11, got12), (got20, got21, got22))
-    pl.semaphore_wait(barrier, len(partners))
+
+    def source(part, where):
+        if part == 2:
+            return rest.at[where]
+        return wide_ref.at[where, slice(part * 256, (part + 1) * 256)]
+
+    halves = (halves0, halves1, halves2)
+    pl.semaphore_wait(barrier, expected)
     pending = []
 
     def start(part, stage, slot, src, dst, who):
@@ -653,25 +684,61 @@
 
     base = [core * 1024 for _ in range(3)]
     flight = {}
-    for slot in (1, 2, 3, 0):
+    for slot in (2, 1, 3, 0):
         for part in range(3):
             quarter, _ = place.along(ORDERS[part][0], slot)
             flight[part, slot] = start(
                 part, 0, slot,
-                source[part].at[rows((1 - core) * 1024 + quarter * 256, 256)],
+                source(part, rows((1 - core) * 1024 + quarter * 256, 256)),
                 pair[part].at[rows(quarter * 256, 256)],
                 place.sibling(),
             )
+    if with_rows:
+        own = pltpu.make_async_copy(rows_ref.at[me], landed_ref.at[me], own_sem)
+        own.start()
+
+        def send(i, carry):
+            other, where = partner(i)
+            pltpu.make_async_remote_copy(
+                src_ref=rows_ref.at[other],
+                dst_ref=landed_ref.at[me],
+                send_sem=row_send,
+                recv_sem=row_recv,
+                device_id=where,
+                device_id_type=MESH,
+            ).start()
+            return carry
+
+        lax.fori_loop(1, OWNERS, send, 0)
     moving = {}
-    for slot in (1, 2, 3, 0):
+
+    def pair_sum(part, slot):
+        quarter, _ = place.along(ORDERS[part][0], slot)
+        flight[part, slot].wait_recv()
+        at = rows(quarter * 256, 256)
+        mine = source(part, rows(core * 1024 + quarter * 256, 256))[...].astype(F32)
+        sums[part][at, :] = (mine + pair[part][at, :].astype(F32)).astype(BF)
+        return quarter * 256
+
+    for part in range(3):
+        at = pair_sum(part, 2)
+        for slot, lead, way in ((0, 0, 1), (2, 128, 3)):
+            who = place.along(ORDERS[part][0], way)[1]
+            src = sums[part].at[rows(at + lead, 128)]
+            moving[part, slot] = start(part, 1, slot, src, halves[part].at[slot // 2], who)
+    for way in (1, 3):
         for part in range(3):
-            quarter, who = place.along(ORDERS[part][0], slot)
-            flight[part, slot].wait_recv()
-            at = rows(quarter * 256, 256)
-            mine = source[part][rows(core * 1024 + quarter * 256, 256), :].astype(F32)
-            sums[part][at, :] = (mine + pair[part][at, :].astype(F32)).astype(BF)
-            if slot:
-                moving[part, slot] = start(part, 1, slot, sums[part].at[at], got[part][0].at[slot - 1], who)
+            at = pair_sum(part, way)
+            slot, lead = (0, 0) if way == 1 else (2, 128)
+            moving[part, slot].wait_recv()
+            piece = rows(at + lead, 128)
+            more = halves[part][slot // 2].astype(F32)
+            sums[part][piece, :] = (sums[part][piece, :].astype(F32) + more).astype(BF)
+            who = place.along(ORDERS[part][0], way)[1]
+            src = sums[part].at[rows(at, 256)]
+            moving[part, way] = start(part, 1, way, src, got[part][0].at[way // 2], who)
+    for part in range(3):
+        pair_sum(part, 0)
     offset = [0, 0, 0]
     for level in range(3):
         size = SIZES[level]
@@ -679,11 +746,12 @@
         for part in range(3):
             mine = place.at[ORDERS[part][level]]
             offset[part] = offset[part] + mine * size
-            for slot in (1, 2, 3):
+            ways = (1, 3) if level == 0 else (1, 2, 3)
+            for slot in ways:
                 moving[part, slot].wait_recv()
             at = rows(offset[part], size)
             value = sums[part][at, :].astype(F32)
-            for slot in range(3):
+            for slot in range(len(ways)):
                 value = value + got[part][level][slot].astype(F32)
             if level < 2:
                 sums[part][at, :] = value.astype(BF)
@@ -709,83 +777,122 @@
                 moving[part, slot].wait_recv()
             where = rows(core * 1024 + offset[part], SIZES[level])
             ref = total[part].at[where]
-            for slot in (1, 2, 3):
+            for slot in (1, 3) if level == 0 else (1, 2, 3):
                 who = place.along(ORDERS[part][level], slot)[1]
-                following[part, slot] = start(part, 6 - level, slot - 0, ref, ref, who)
+                following[part, slot] = start(part, 6 - level, slot, ref, ref, who)
             if level == 0:
                 final.append(start(part, 7, 0, ref, ref, place.sibling()))
         moving = following
-    for slot in (1, 3, 2):
+
+    def piece_of(part, way, lead, size):
+        quarter = place.along(ORDERS[part][0], way)[0]
+        return total[part].at[rows(core * 1024 + quarter * 256 + lead, size)]
+
+    for way in (1, 3):
         for part in range(3):
-            moving[part, slot].wait_recv()
-            quarter = place.along(ORDERS[part][0], 4 - slot)[0]
-            ref = total[part].at[rows(core * 1024 + quarter * 256, 256)]
-            final.append(start(part, 7, slot, ref, ref, place.sibling()))
+            moving[part, way].wait_recv()
+            slot, lead = (0, 0) if way == 1 else (2, 128)
+            ref = piece_of(part, 4 - way, lead, 128)
+            who = place.along(ORDERS[part][0], way)[1]
+            moving[part, slot] = start(part, 6, slot, ref, ref, who)
+            ref = piece_of(part, 4 - way, 0, 256)
+            final.append(start(part, 7, way, ref, ref, place.sibling()))
+    for part in range(3):
+        moving[part, 0].wait_recv()
+        moving[part, 2].wait_recv()
+        ref = piece_of(part, 2, 0, 256)
+        final.append(start(part, 7, 2, ref, ref, place.sibling()))
     for copy in final:
         copy.wait_recv()
     for copy in pending:
         copy.wait_send()
-
-
-def reduce_all(first_part, proj_grad, last_part, out_grad, ident):
+    if with_rows:
+        whole = pltpu.make_async_remote_copy(
+            src_ref=rows_ref.at[pl.ds(0, OWNERS - 1)],
+            dst_ref=landed_ref.at[pl.ds(0, OWNERS - 1)],
+            send_sem=row_send,
+            recv_sem=row_recv,
+            device_id=partner(1)[1],
+            device_id_type=MESH,
+        )
+        whole.wait_send()
+        whole.wait_recv()
+        own.wait()
+
+
+def reduce_all(wide, extra, ident, row_blocks=None):
     vm = pltpu.VMEM
-    widths = (512, 512, 384)
-    return pl.pallas_call(
-        reduce_kernel,
-        out_shape=tuple(jax.ShapeDtypeStruct((2048, w), BF) for w in widths),
-        in_specs=[pl.BlockSpec(memory_space=vm)] * 4,
-        out_specs=tuple(pl.BlockSpec(memory_space=vm) for _ in widths),
-        scratch_shapes=[vm((2048, 384), BF)]
+    with_rows = row_blocks is not None
+    widths = (256, 256, 128 if with_rows else 256)
+    out_shape = tuple(jax.ShapeDtypeStruct((2048, w), BF) for w in widths)
+    scratch = (
+        [vm((2048, widths[2]), BF)]
         + [vm((1024, w), BF) for w in widths]
         + [vm((1024, w), BF) for w in widths]
         + [vm((3, size, w), BF) for w in widths for size in SIZES]
-        + [pltpu.SemaphoreType.DMA((3, 8, 4))] * 2,
+        + [vm((2, 128, w), BF) for w in widths]
+        + [pltpu.SemaphoreType.DMA((3, 8, 4))] * 2
+    )
+    operands = (wide, extra)
+    if with_rows:
+        out_shape = (jax.ShapeDtypeStruct(row_blocks.shape, BF),) + out_shape
+        operands = (row_blocks,) + operands
+        scratch += [pltpu.SemaphoreType.DMA] * 3
+    return pl.pallas_call(
+        functools.partial(reduce_kernel, with_rows),
+        out_shape=out_shape,
+        in_specs=[pl.BlockSpec(memory_space=vm) for _ in operands],
+        out_specs=tuple(pl.BlockSpec(memory_space=vm) for _ in out_shape),
+        scratch_shapes=scratch,
         compiler_params=pltpu.CompilerParams(
             collective_id=ident, has_side_effects=True, vmem_limit_bytes=VMEM_LIMIT
         ),
-        name="reduce_all",
-    )(first_part, proj_grad, last_part, out_grad)
-
-
-def widen_kernel(a_ref, b_ref, c_ref, first_ref, last_ref, proj_ref, out_ref):
-    step = pl.program_id(0)
-    first_ref[...] = a_ref[...].astype(F32)
-    proj_ref[...] = b_ref[...].astype(F32)
-    block0 = step * 3
-    for k in range(3):
-        block = block0 + k
-        value = c_ref[:, k * 128 : (k + 1) * 128].astype(F32)
-        for lane in range(4):
-
-            @pl.when((block < 8) & (block % 4 == lane))
-            def _():
-                last_ref[pl.ds(pl.multiple_of((block // 4) * 512, 512), 512), lane * 128 : (lane + 1) * 128] = value
-
-            @pl.when((block >= 8) & (block % 4 == lane))
-            def _():
-                out_ref[:, lane * 128 : (lane + 1) * 128] = value
-
-
-def widen(a, b, c):
-    return pl.pallas_call(
+        name="rows_and_weights" if with_rows else "reduce_cores",
+    )(*operands)
+
+
+def widen_kernel(p0, p1, p2, c0, c1, c2, first_ref, last_ref, proj_ref, out_ref):
+    first_ref[:, 0:256] = c0[...].astype(F32)
+    first_ref[:, 256:512] = c1[...].astype(F32)
+    for block in range(4):
+        lanes = slice(block * 512, block * 512 + 256)
+        proj_ref[:, lanes] = p0[block].astype(F32)
+        lanes = slice(block * 512 + 256, block * 512 + 512)
+        proj_ref[:, lanes] = p1[block].astype(F32)
+        out_ref[:, block * 128 : (block + 1) * 128] = p2[block].astype(F32)
+        last_ref[block // 2, :, (block % 2) * 256 : (block % 2 + 1) * 256] = c2[block].astype(F32)
+
+
+def widen(weights, cores):
+    steps = 4
+    rows = 512 // steps
+    p0, p1, p2 = (x.reshape(4, 512, x.shape[1]) for x in weights)
+    c0, c1, c2 = cores
+
+    def cut(width):
+        return pl.BlockSpec((4, rows, width), lambda i: (0, i, 0))
+
+    flat = pl.BlockSpec((4 * rows, 256), lambda i: (i, 0))
+    first, last, proj, out = pl.pallas_call(
         widen_kernel,
-        grid=(4,),
-        in_specs=[pl.BlockSpec((512, w), lambda i: (i, 0)) for w in (512, 512, 384)],
+        grid=(steps,),
+        in_specs=[cut(256), cut(256), cut(128), flat, flat, cut(256)],
         out_specs=(
-            pl.BlockSpec((512, 512), lambda i: (i, 0)),
-            pl.BlockSpec((1024, 512), lambda i: (0, 0)),
-            pl.BlockSpec((512, 512), lambda i: (0, i)),
-            pl.BlockSpec((512, 512), lambda i: (0, 0)),
+            pl.BlockSpec((4 * rows, 512), lambda i: (i, 0)),
+            pl.BlockSpec((2, rows, 512), lambda i: (0, i, 0)),
+            pl.BlockSpec((rows, 2048), lambda i: (i, 0)),
+            pl.BlockSpec((rows, 512), lambda i: (i, 0)),
         ),
         out_shape=(
             jax.ShapeDtypeStruct((2048, 512), F32),
-            jax.ShapeDtypeStruct((1024, 512), F32),
+            jax.ShapeDtypeStruct((2, 512, 512), F32),
             jax.ShapeDtypeStruct((512, 2048), F32),
             jax.ShapeDtypeStruct((512, 512), F32),
         ),
         compiler_params=pltpu.CompilerParams(vmem_limit_bytes=VMEM_LIMIT),
         name="widen",
-    )(a, b, c)
+    )(p0, p1, p2, c0, c1, c2.reshape(4, 512, 256))
+    return first, last.reshape(1024, 512), proj, out
 
 
 def exchange(x):
@@ -798,10 +905,10 @@
     built, spread, part, lt = build(arrived, first_core, middle_core, last_core)
     recv = exchange(built)
     layer_rows, sent, proj_grad, out_grad = layer(recv, slot_row, slot_col, w_proj, w_out, layer_grad)
-    tiles = exchange(sent)
+    tiles, *weights = reduce_all(proj_grad, out_grad, 2, sent)
     first_part, grad_middle, last_part = core_grads(arrived, tiles, spread, part, lt, middle_core)
-    totals = reduce_all(first_part, proj_grad, last_part, out_grad, 2)
-    grad_first, grad_last, proj_total, out_total = widen(*totals)
+    cores = reduce_all(first_part, last_part, 3)
+    grad_first, grad_last, proj_total, out_total = widen(weights, cores)
     return (layer_rows, grad_first, grad_middle, grad_last, proj_total, out_total)
 
 

time: 224 us -> 239 us (1.067)
  Pallas kernels: 172 us -> 212 us
  blocking collectives: 50.8 us -> 26.1 us
    pallas_call x2 -> x3, Pallas kernels: 65.3 us -> 109 us  [the longest x2 102 us: reduce_all(): pl.pallas_call(functools.partial(reduce_kernel, with_rows), out_shape=out...]
    all_to_all x2 -> x1, blocking collectives: 50.8 us -> 26.1 us  [exchange(): return lax.all_to_all(x, AXES, split_axis=0, concat_axis=0, tiled=True)]
    pallas_call x1, Pallas kernels: 33.1 us -> 29.3 us  [layer(): pl.pallas_call(layer_kernel, out_shape=(jax.ShapeDtypeStruct((EVENTS, 512...]
where the time goes in v3:
time: 239 us
  Pallas kernels  212 us (89%)
  blocking collectives  26.1 us (11%)
    pallas_call x2, Pallas kernels, reduce_all(): pl.pallas_call(functools.partial(reduce_kernel, with_rows), out_shape=out...  102 us
    pallas_call x1, Pallas kernels, core_grads(): pl.pallas_call(core_grad_kernel, grid=(2,), in_specs=[pl.BlockSpec((OWNER...  30.6 us
    pallas_call x1, Pallas kernels, layer(): pl.pallas_call(layer_kernel, out_shape=(jax.ShapeDtypeStruct((EVENTS, 512...  29.3 us
    all_to_all x1, blocking collectives, exchange(): return lax.all_to_all(x, AXES, split_axis=0, concat_axis=0, tiled=True)  26.1 us
    pallas_call x1, Pallas kernels, build(): pl.pallas_call(build_kernel, grid=(2,), in_specs=[pl.BlockSpec((OWNERS, 1...  25.6 us
    pallas_call x1, Pallas kernels, prep(): pl.pallas_call(prep_kernel, out_shape=(jax.ShapeDtypeStruct((16, 8, 1, 12...  17.7 us
    pallas_call x1, Pallas kernels, widen(): pl.pallas_call(widen_kernel, grid=(steps,), in_specs=[cut(256), cut(256),...  7.17 us

profile of v3, /device:TPU:1, one launch (start us, length us, event | category | flops | bytes accessed | tf_op | source)
XLA Modules:
  0.0 239.1 jit_solution(17266812651921628710)
XLA Ops:
  0.6 17.7 %prep.1 = (s32[16,8,1,128]{3,2,1,0:T(1,128)}, s32[8,512]{1,0:T(8,128)}, s32[512,128]{1,0:T(8,128)}) custom-call(s32[3,512]{1,0:T(4,128)} %dig_ref.1), custom_call_target="tpu_custom_call" | custom-call | tf_op jit(solution)/shard_map/prep/pallas_call | solution.py:105
  18.3 25.6 %build.1 = (bf16[128,2,16,128]{3,2,1,0:T(8,128)(2,1)}, bf16[8192,256]{1,0:T(8,128)(2,1)}, bf16[256,64,256]{2,1,0:T(8,128)(2,1)}, bf16[256,32,256]{2,1,0:T(8,128)(2,1)}) custom-call(s32[128,1,128]{2,1,0:T(1,128)} %bitcast.10, bf16[2048,512]{1,0:T(8,128)(2,1)} %first_ref.1, bf16[256,512]{1,0:T(8,128)(2,1)} %middle_ref.3, bf16[1024,512]{1,0:T(8,128)(2,1)} %last_ref.1), custom_call_target="tpu_custom_call" | custom-call | tf_op jit(solution)/shard_map/build/pallas_call | solution.py:215
  43.9 26.1 %all_to_all.5.recv_ref = bf16[128,2,16,128]{3,2,1,0:T(8,128)(2,1)} all-to-all(bf16[128,2,16,128]{3,2,1,0:T(8,128)(2,1)} %get-tuple-element.32), channel_id=1, replica_groups=mesh['dp'=16,'cores'=8] {'dp','cores'}, dimensions={0} | all-to-all | bytes 2097152 | tf_op jit(solution)/shard_map/all_to_all | solution.py:899
  70.0 29.3 %layer.1 = (bf16[512,512]{1,0:T(8,128)(2,1)}, bf16[128,2,16,128]{3,2,1,0:T(8,128)(2,1)}, bf16[2048,512]{1,0:T(8,128)(2,1)}, bf16[512,512]{1,0:T(8,128)(2,1)}) custom-call(bf16[128,2,16,128]{3,2,1,0:T(8,128)(2,1)} %all_to_all.5.recv_ref, s32[8,512]{1,0:T(8,128)} %get-tuple-element.33.slot_row_ref, s32[512,128]{1,0:T(8,128)} %get-tuple-element.34.slot_col_ref, ...), custom_call_target="tpu_custom_call" | custom-call | tf_op jit(solution)/shard_map/layer/pallas_call | solution.py:422
  99.3 58.3 %rows_and_weights.1 = (bf16[128,2,16,128]{3,2,1,0:T(8,128)(2,1)}, bf16[2048,256]{1,0:T(8,128)(2,1)}, bf16[2048,256]{1,0:T(8,128)(2,1)}, bf16[2048,128]{1,0:T(8,128)(2,1)}) custom-call(bf16[128,2,16,128]{3,2,1,0:T(8,128)(2,1)} %get-tuple-element.36.refs_0_, bf16[2048,512]{1,0:T(8,128)(2,1)} %get-tuple-element.37.refs_1_, ...), custom_call_target="tpu_custom_call" | custom-call | tf_op jit(solution)/shard_map/rows_and_weights/pallas_call | solution.py:841
  157.6 30.6 %core_grads.1 = (bf16[2048,512]{1,0:T(8,128)(2,1)}, f32[256,512]{1,0:T(8,128)}, bf16[1024,512]{1,0:T(8,128)(2,1)}) custom-call(s32[128,1,128]{2,1,0:T(1,128)} %bitcast.11, bf16[128,2,16,128]{3,2,1,0:T(8,128)(2,1)} %get-tuple-element.42.tile_ref, bf16[8192,256]{1,0:T(8,128)(2,1)} %get-tuple-element.43.spread_ref, ...), custom_call_target="tpu_custom_call" | custom-call | tf_op jit(solution)/shard_map/core_grads/pallas_call | solution.py:557
  188.3 43.6 %reduce_cores.1 = (bf16[2048,256]{1,0:T(8,128)(2,1)}, bf16[2048,256]{1,0:T(8,128)(2,1)}, bf16[2048,256]{1,0:T(8,128)(2,1)}) custom-call(bf16[2048,512]{1,0:T(8,128)(2,1)} %get-tuple-element.46.refs_0_, bf16[1024,512]{1,0:T(8,128)(2,1)} %get-tuple-element.47.refs_1_), custom_call_target="tpu_custom_call" | custom-call | tf_op jit(solution)/shard_map/reduce_cores/pallas_call | solution.py:841
  231.9 7.2 %widen.1 = (f32[2048,512]{1,0:T(8,128)}, f32[2,512,512]{2,1,0:T(8,128)}, f32[512,2048]{1,0:T(8,128)}, f32[512,512]{1,0:T(8,128)}) custom-call(bf16[4,512,256]{2,1,0:T(8,128)(2,1)} %bitcast.6, bf16[4,512,256]{2,1,0:T(8,128)(2,1)} %bitcast.7, bf16[4,512,128]{2,1,0:T(8,128)(2,1)} %bitcast.9, bf16[2048,256]{1,0:T(8,128)(2,1)} %get-tuple-element.48.c0, ...), custom_call_target="tpu_custom_call" | custom-call | tf_op jit(solution)/shard_map/widen/pallas_call | solution.py:876

commit v4 on v3

--- a/solution.py
+++ b/solution.py
@@ -180,7 +180,7 @@
 
     lax.fori_loop(0, 8, spread_step, 0)
 
-    group = 16
+    group = 128
     low = low_lanes((group * 8, 128))
 
     def combine(i, carry):
@@ -263,8 +263,9 @@
     rows_ref, sent_ref, dproj_ref, dout_ref,
     tiles, slots, emb, normed, y_in, z, act, mixed, y_mid, gated, dz, dmixed, work, work_v, work_k, sc_in,
 ):
-    low = low_lanes((256 // 2, 128))
-    step = 128
+    low = low_lanes((128, 128))
+    step = 256
+    tall = 512
 
     def widen(i, carry):
         srcs = pl.ds(pl.multiple_of(i * 32, 32), 32)
@@ -290,10 +291,10 @@
     emb[...] = dot(dot(pick, slots[...]).astype(BF), flip)
 
     def project(i, carry):
-        at = pl.ds(pl.multiple_of(i * step, step), step)
+        at = pl.ds(pl.multiple_of(i * tall, tall), tall)
         y, scale = norm_stats(emb[at, :])
         y_in[at, :] = y
-        sc_in[at, :] = jnp.broadcast_to(scale, (step, 128))
+        sc_in[at, :] = jnp.broadcast_to(scale, (tall, 128))
         normed[at, :] = y.astype(BF)
         for block in range(4):
             lanes = slice(block * 512, (block + 1) * 512)
@@ -302,7 +303,7 @@
             act[at, lanes] = (value * sigmoid(value)).astype(BF)
         return carry
 
-    lax.fori_loop(0, EVENTS // step, project, 0)
+    lax.fori_loop(0, EVENTS // tall, project, 0)
     scaling = 1.0 / math.sqrt(128.0)
 
     def scores_of(head, block):
@@ -315,7 +316,7 @@
 
     def attend(head, carry):
         cols = pl.ds(pl.multiple_of(head * 128, 128), 128)
-        for block in range(4):
+        for block in range(2):
             end = (block + 1) * step
             s, causal = scores_of(head, block)
             weights = jnp.where(causal, s * sigmoid(s), 0.0).astype(BF)
@@ -326,7 +327,7 @@
     lax.fori_loop(0, 4, attend, 0)
 
     def finish(i, carry):
-        at = pl.ds(pl.multiple_of(i * step, step), step)
+        at = pl.ds(pl.multiple_of(i * tall, tall), tall)
         y, scale = norm_stats(mixed[at, :])
         u = act[at, 0:512].astype(F32)
         gate = (y * u).astype(BF)
@@ -341,7 +342,7 @@
         dmixed[at, :] = norm_grad(d_gate * u, y, scale).astype(BF)
         return carry
 
-    lax.fori_loop(0, EVENTS // step, finish, 0)
+    lax.fori_loop(0, EVENTS // tall, finish, 0)
     dout_ref[...] = dot(gated[...], grad_ref[...], 0, 0).astype(BF)
 
     def attend_grad(head, carry):
@@ -349,7 +350,7 @@
         vcols = pl.ds(pl.multiple_of(512 + head * 128, 128), 128)
         qcols = pl.ds(pl.multiple_of(1024 + head * 128, 128), 128)
         kcols = pl.ds(pl.multiple_of(1536 + head * 128, 128), 128)
-        for block in (3, 2, 1, 0):
+        for block in (1, 0):
             end = (block + 1) * step
             rows = slice(block * step, end)
             s, causal = scores_of(head, block)
@@ -360,7 +361,7 @@
             d_s = jnp.where(causal, d_w * (sig * (1.0 + s * (1.0 - sig))) * scaling, 0.0).astype(BF)
             v_part = dot(weights, dm, 0, 0)
             k_part = dot(d_s, act[rows, qcols], 0, 0)
-            if block == 3:
+            if block == 1:
                 work_v[...] = v_part
                 work_k[...] = k_part
             else:
@@ -387,13 +388,13 @@
     back = one_hot(source == (target % 8) * 64 + ((target // 8) % 8) * 8 + target // 64)
 
     def close(i, carry):
-        at = pl.ds(pl.multiple_of(i * step, step), step)
+        at = pl.ds(pl.multiple_of(i * tall, tall), tall)
         d_normed = dot(dz[at, :], proj_ref[...], 1, 1).astype(BF).astype(F32)
         d_rows = norm_grad(d_normed, y_in[at, :], sc_in[at, 0:1]) + grad_ref[at, :].astype(F32)
         gated[at, :] = d_rows.astype(BF)
         return carry
 
-    lax.fori_loop(0, EVENTS // step, close, 0)
+    lax.fori_loop(0, EVENTS // tall, close, 0)
     turned = dot(gated[...], back).astype(BF)
     for half in range(2):
         for tlo in range(2):
@@ -453,14 +454,14 @@
 def core_grad_kernel(
     arrived_ref, tile_ref, spread_ref, part_ref, lt_ref, middle_ref,
     first_out, middle_out, last_out,
-    flipped, pg, ls, ss, fterm, lterm, first_acc, last_acc,
+    flipped, pg, ls, ss, fterm, lterm,
 ):
     half = pl.program_id(0)
     arrived = arrived_ref[...].reshape(OWNERS, 128)
     flipped[...] = jnp.transpose(arrived.astype(F32)).astype(I32) - 1
     _, middle_col, _ = index_columns(arrived, half)
     mask0, mask1 = slice_masks(middle_col)
-    group = 16
+    group = 128
     low = low_lanes((group, 8, 128))
     own = (iota((group, 16, 128), 1) // 8) == (iota((group, 16, 128), 2) // 64)
 
@@ -497,6 +498,7 @@
         ss[0] = back[:, 0:128]
         ss[1] = back[:, 128:256]
         rows = slice(t * 128, (t + 1) * 128)
+        keep = pl.ds(pl.multiple_of(half * 512 + t * 128, 128), 128)
         m0, m1 = mask0[rows], mask1[rows]
         for pair in range(4):
             lanes = slice(pair * 128, (pair + 1) * 128)
@@ -505,51 +507,47 @@
                 where = pl.ds(pair * 2 + odd, 128, stride=8)
                 x = jnp.where(m0, ss[0, where, :], 0.0) + jnp.where(m1, ss[1, where, :], 0.0)
                 found.append(x + half_turn(x))
-            fterm[rows, lanes] = jnp.where(low, found[0], found[1]).astype(BF)
+            fterm[keep, lanes] = jnp.where(low, found[0], found[1]).astype(BF)
             base = (t % 2) * 8 + pair * 2
             y0 = ls[t // 2, pl.ds(base, 128, stride=16), :]
             y1 = ls[t // 2, pl.ds(base + 1, 128, stride=16), :]
-            lterm[rows, lanes] = jnp.where(low, y0, y1).astype(BF)
+            lterm[keep, lanes] = jnp.where(low, y0, y1).astype(BF)
 
     source = iota((512, 512), 0)
     perm = one_hot(iota((512, 512), 1) == (source % 64) * 8 + source // 64)
-    lterm[...] = dot(lterm[...], perm).astype(BF)
+    done = pl.ds(pl.multiple_of(half * 512, 512), 512)
+    lterm[done, :] = dot(lterm[done, :], perm).astype(BF)
 
     def index_row(digit):
-        return jnp.concatenate([flipped[pl.ds(digit * 8 + half * 4 + t, 1), :] for t in range(4)], axis=1)
-
-    first_row = index_row(0)
-    last_row = index_row(2)
+        return jnp.concatenate([flipped[digit * 8 + t : digit * 8 + t + 1, :] for t in range(8)], axis=1)
 
     @pl.when(half == 0)
     def _():
         middle_out[...] = middle_part
-        first_acc[...] = jnp.zeros_like(first_acc)
-        last_acc[...] = jnp.zeros_like(last_acc)
 
     @pl.when(half == 1)
     def _():
         middle_out[...] += middle_part
 
-    def scatter_first(i, carry):
-        at = pl.ds(pl.multiple_of(i * 256, 256), 256)
-        place = one_hot(iota((256, 512), 0) + i * 256 == first_row)
-        first_acc[at, :] += dot(place, fterm[...])
-        return carry
-
-    def scatter_last(i, carry):
-        at = pl.ds(pl.multiple_of(i * 256, 256), 256)
-        place = one_hot(iota((256, 512), 0) + i * 256 == last_row)
-        last_acc[at, :] += dot(place, lterm[...])
-        return carry
-
-    lax.fori_loop(0, 8, scatter_first, 0)
-    lax.fori_loop(0, 4, scatter_last, 0)
-
     @pl.when(half == 1)
     def _():
-        first_out[...] = first_acc[...].astype(BF)
-        last_out[...] = last_acc[...].astype(BF)
+        first_row = index_row(0)
+        last_row = index_row(2)
+
+        def scatter_first(i, carry):
+            at = pl.ds(pl.multiple_of(i * 256, 256), 256)
+            place = one_hot(iota((256, 1024), 0) + i * 256 == first_row)
+            first_out[at, :] = dot(place, fterm[...]).astype(BF)
+            return carry
+
+        def scatter_last(i, carry):
+            at = pl.ds(pl.multiple_of(i * 256, 256), 256)
+            place = one_hot(iota((256, 1024), 0) + i * 256 == last_row)
+            last_out[at, :] = dot(place, lterm[...]).astype(BF)
+            return carry
+
+        lax.fori_loop(0, 8, scatter_first, 0)
+        lax.fori_loop(0, 4, scatter_last, 0)
 
 
 def core_grads(arrived, tiles, spread, part, lt, middle_core):
@@ -580,10 +578,8 @@
             vm((4096, 512), BF),
             vm((2, 2048, 128), F32),
             vm((2, 1024, 128), F32),
-            vm((512, 512), BF),
-            vm((512, 512), BF),
-            vm((2048, 512), F32),
-            vm((1024, 512), F32),
+            vm((1024, 512), BF),
+            vm((1024, 512), BF),
         ],
         compiler_params=pltpu.CompilerParams(vmem_limit_bytes=VMEM_LIMIT),
         name="core_grads",
@@ -612,58 +608,33 @@
 
 
 def reduce_kernel(
-    with_rows, *refs,
+    first_ref, proj_ref, last_ref, out_ref,
+    total0, total1, total2,
+    rest, pair0, pair1, pair2, sum0, sum1, sum2,
+    got00, got01, got02, got10, got11, got12, got20, got21, got22,
+    halves0, halves1, halves2, send_sem, recv_sem,
 ):
-    if with_rows:
-        rows_ref, refs = refs[0], refs[1:]
-    wide_ref, extra_ref = refs[:2]
-    refs = refs[2:]
-    if with_rows:
-        landed_ref, refs = refs[0], refs[1:]
-    total0, total1, total2, rest, pair0, pair1, pair2, sum0, sum1, sum2 = refs[:10]
-    got00, got01, got02, got10, got11, got12, got20, got21, got22 = refs[10:19]
-    halves0, halves1, halves2, send_sem, recv_sem = refs[19:24]
     place = Place()
     core = place.core
     barrier = pltpu.get_barrier_semaphore()
-    if with_rows:
-        row_send, row_recv, own_sem = refs[24:]
-        me = lax.axis_index("dp") * 8 + lax.axis_index("cores")
-
-        def partner(i):
-            other = lax.rem(me + i, OWNERS)
-            return other, (other // 8, lax.rem(other, 8))
-
-        def greet(i, carry):
-            pl.semaphore_signal(barrier, inc=1, device_id=partner(i)[1], device_id_type=MESH)
-            return carry
-
-        lax.fori_loop(1, OWNERS, greet, 0)
-        expected = OWNERS - 1
-    else:
-        partners = [place.sibling()] + [place.along(d, o)[1] for d in range(3) for o in (1, 2, 3)]
-        for who in partners:
-            pl.semaphore_signal(barrier, inc=1, device_id=who, device_id_type=MESH)
-        expected = len(partners)
-    width = rest.shape[1]
-    for block in range(4):
-        if with_rows:
-            value = extra_ref[:, block * 128 : (block + 1) * 128]
+    partners = [place.sibling()] + [place.along(d, o)[1] for d in range(3) for o in (1, 2, 3)]
+    for who in partners:
+        pl.semaphore_signal(barrier, inc=1, device_id=who, device_id_type=MESH)
+    for block in range(12):
+        row = (block // 3) * 512
+        lanes = slice((block % 3) * 128, (block % 3 + 1) * 128)
+        if block < 8:
+            value = last_ref[(block // 4) * 512 : (block // 4 + 1) * 512, (block % 4) * 128 : (block % 4 + 1) * 128]
         else:
-            value = extra_ref[(block // 2) * 512 : (block // 2 + 1) * 512, (block % 2) * 256 : (block % 2 + 1) * 256]
-        rest[block * 512 : (block + 1) * 512, :] = value
+            value = out_ref[:, (block % 4) * 128 : (block % 4 + 1) * 128]
+        rest[row : row + 512, lanes] = value
+    source = (first_ref, proj_ref, rest)
     total = (total0, total1, total2)
     pair = (pair0, pair1, pair2)
     sums = (sum0, sum1, sum2)
     got = ((got00, got01, got02), (got10, got11, got12), (got20, got21, got22))
-
-    def source(part, where):
-        if part == 2:
-            return rest.at[where]
-        return wide_ref.at[where, slice(part * 256, (part + 1) * 256)]
-
     halves = (halves0, halves1, halves2)
-    pl.semaphore_wait(barrier, expected)
+    pl.semaphore_wait(barrier, len(partners))
     pending = []
 
     def start(part, stage, slot, src, dst, who):
@@ -689,34 +660,17 @@
             quarter, _ = place.along(ORDERS[part][0], slot)
             flight[part, slot] = start(
                 part, 0, slot,
-                source(part, rows((1 - core) * 1024 + quarter * 256, 256)),
+                source[part].at[rows((1 - core) * 1024 + quarter * 256, 256)],
                 pair[part].at[rows(quarter * 256, 256)],
                 place.sibling(),
             )
-    if with_rows:
-        own = pltpu.make_async_copy(rows_ref.at[me], landed_ref.at[me], own_sem)
-        own.start()
-
-        def send(i, carry):
-            other, where = partner(i)
-            pltpu.make_async_remote_copy(
-                src_ref=rows_ref.at[other],
-                dst_ref=landed_ref.at[me],
-                send_sem=row_send,
-                recv_sem=row_recv,
-                device_id=where,
-                device_id_type=MESH,
-            ).start()
-            return carry
-
-        lax.fori_loop(1, OWNERS, send, 0)
     moving = {}
 
     def pair_sum(part, slot):
         quarter, _ = place.along(ORDERS[part][0], slot)
         flight[part, slot].wait_recv()
         at = rows(quarter * 256, 256)
-        mine = source(part, rows(core * 1024 + quarter * 256, 256))[...].astype(F32)
+        mine = source[part][rows(core * 1024 + quarter * 256, 256), :].astype(F32)
         sums[part][at, :] = (mine + pair[part][at, :].astype(F32)).astype(BF)
         return quarter * 256
 
@@ -806,77 +760,54 @@
         copy.wait_recv()
     for copy in pending:
         copy.wait_send()
-    if with_rows:
-        whole = pltpu.make_async_remote_copy(
-            src_ref=rows_ref.at[pl.ds(0, OWNERS - 1)],
-            dst_ref=landed_ref.at[pl.ds(0, OWNERS - 1)],
-            send_sem=row_send,
-            recv_sem=row_recv,
-            device_id=partner(1)[1],
-            device_id_type=MESH,
-        )
-        whole.wait_send()
-        whole.wait_recv()
-        own.wait()
-
-
-def reduce_all(wide, extra, ident, row_blocks=None):
+
+
+def reduce_all(first_part, proj_grad, last_part, out_grad, ident):
     vm = pltpu.VMEM
-    with_rows = row_blocks is not None
-    widths = (256, 256, 128 if with_rows else 256)
-    out_shape = tuple(jax.ShapeDtypeStruct((2048, w), BF) for w in widths)
-    scratch = (
-        [vm((2048, widths[2]), BF)]
+    widths = (512, 512, 384)
+    return pl.pallas_call(
+        reduce_kernel,
+        out_shape=tuple(jax.ShapeDtypeStruct((2048, w), BF) for w in widths),
+        in_specs=[pl.BlockSpec(memory_space=vm)] * 4,
+        out_specs=tuple(pl.BlockSpec(memory_space=vm) for _ in widths),
+        scratch_shapes=[vm((2048, 384), BF)]
         + [vm((1024, w), BF) for w in widths]
         + [vm((1024, w), BF) for w in widths]
         + [vm((3, size, w), BF) for w in widths for size in SIZES]
         + [vm((2, 128, w), BF) for w in widths]
-        + [pltpu.SemaphoreType.DMA((3, 8, 4))] * 2
-    )
-    operands = (wide, extra)
-    if with_rows:
-        out_shape = (jax.ShapeDtypeStruct(row_blocks.shape, BF),) + out_shape
-        operands = (row_blocks,) + operands
-        scratch += [pltpu.SemaphoreType.DMA] * 3
-    return pl.pallas_call(
-        functools.partial(reduce_kernel, with_rows),
-        out_shape=out_shape,
-        in_specs=[pl.BlockSpec(memory_space=vm) for _ in operands],
-        out_specs=tuple(pl.BlockSpec(memory_space=vm) for _ in out_shape),
-        scratch_shapes=scratch,
+        + [pltpu.SemaphoreType.DMA((3, 8, 4))] * 2,
         compiler_params=pltpu.CompilerParams(
             collective_id=ident, has_side_effects=True, vmem_limit_bytes=VMEM_LIMIT
         ),
-        name="rows_and_weights" if with_rows else "reduce_cores",
-    )(*operands)
-
-
-def widen_kernel(p0, p1, p2, c0, c1, c2, first_ref, last_ref, proj_ref, out_ref):
-    first_ref[:, 0:256] = c0[...].astype(F32)
-    first_ref[:, 256:512] = c1[...].astype(F32)
+        name="reduce_all",
+    )(first_part, proj_grad, last_part, out_grad)
+
+
+def widen_kernel(a_ref, b_ref, c_ref, first_ref, last_ref, proj_ref, out_ref):
+    first_ref[...] = a_ref[...].astype(F32)
     for block in range(4):
-        lanes = slice(block * 512, block * 512 + 256)
-        proj_ref[:, lanes] = p0[block].astype(F32)
-        lanes = slice(block * 512 + 256, block * 512 + 512)
-        proj_ref[:, lanes] = p1[block].astype(F32)
-        out_ref[:, block * 128 : (block + 1) * 128] = p2[block].astype(F32)
-        last_ref[block // 2, :, (block % 2) * 256 : (block % 2 + 1) * 256] = c2[block].astype(F32)
-
-
-def widen(weights, cores):
-    steps = 4
+        lanes = slice(block * 512, (block + 1) * 512)
+        proj_ref[:, lanes] = b_ref[block].astype(F32)
+    for block in range(12):
+        value = c_ref[block // 3, :, (block % 3) * 128 : (block % 3 + 1) * 128].astype(F32)
+        lanes = slice((block % 4) * 128, (block % 4 + 1) * 128)
+        if block < 8:
+            last_ref[block // 4, :, lanes] = value
+        else:
+            out_ref[:, lanes] = value
+
+
+def widen(a, b, c):
+    steps = 8
     rows = 512 // steps
-    p0, p1, p2 = (x.reshape(4, 512, x.shape[1]) for x in weights)
-    c0, c1, c2 = cores
-
-    def cut(width):
-        return pl.BlockSpec((4, rows, width), lambda i: (0, i, 0))
-
-    flat = pl.BlockSpec((4 * rows, 256), lambda i: (i, 0))
     first, last, proj, out = pl.pallas_call(
         widen_kernel,
         grid=(steps,),
-        in_specs=[cut(256), cut(256), cut(128), flat, flat, cut(256)],
+        in_specs=[
+            pl.BlockSpec((4 * rows, 512), lambda i: (i, 0)),
+            pl.BlockSpec((4, rows, 512), lambda i: (0, i, 0)),
+            pl.BlockSpec((4, rows, 384), lambda i: (0, i, 0)),
+        ],
         out_specs=(
             pl.BlockSpec((4 * rows, 512), lambda i: (i, 0)),
             pl.BlockSpec((2, rows, 512), lambda i: (0, i, 0)),
@@ -891,7 +822,7 @@
         ),
         compiler_params=pltpu.CompilerParams(vmem_limit_bytes=VMEM_LIMIT),
         name="widen",
-    )(p0, p1, p2, c0, c1, c2.reshape(4, 512, 256))
+    )(a, b.reshape(4, 512, 512), c.reshape(4, 512, 384))
     return first, last.reshape(1024, 512), proj, out
 
 
@@ -905,10 +836,10 @@
     built, spread, part, lt = build(arrived, first_core, middle_core, last_core)
     recv = exchange(built)
     layer_rows, sent, proj_grad, out_grad = layer(recv, slot_row, slot_col, w_proj, w_out, layer_grad)
-    tiles, *weights = reduce_all(proj_grad, out_grad, 2, sent)
+    tiles = exchange(sent)
     first_part, grad_middle, last_part = core_grads(arrived, tiles, spread, part, lt, middle_core)
-    cores = reduce_all(first_part, last_part, 3)
-    grad_first, grad_last, proj_total, out_total = widen(weights, cores)
+    totals = reduce_all(first_part, proj_grad, last_part, out_grad, 2)
+    grad_first, grad_last, proj_total, out_total = widen(*totals)
     return (layer_rows, grad_first, grad_middle, grad_last, proj_total, out_total)
 
 

time: 239 us -> 200 us (0.84)
  Pallas kernels: 212 us -> 148 us
  blocking collectives: 26.1 us -> 50.8 us
    pallas_call x3 -> x2, Pallas kernels: 109 us -> 62.9 us  [the longest x1 54.7 us: reduce_all(): pl.pallas_call(reduce_kernel, out_shape=tuple((jax.ShapeDtypeStruct((2048...]
    all_to_all x1 -> x2, blocking collectives: 26.1 us -> 50.8 us  [exchange(): return lax.all_to_all(x, AXES, split_axis=0, concat_axis=0, tiled=True)]
    pallas_call x1, Pallas kernels: 30.6 us -> 22.7 us  [core_grads(): pl.pallas_call(core_grad_kernel, grid=(2,), in_specs=[pl.BlockSpec((OWNER...]
    pallas_call x1, Pallas kernels: 29.3 us -> 22.3 us  [layer(): pl.pallas_call(layer_kernel, out_shape=(jax.ShapeDtypeStruct((EVENTS, 512...]
    pallas_call x1, Pallas kernels: 25.6 us -> 22.6 us  [build(): pl.pallas_call(build_kernel, grid=(2,), in_specs=[pl.BlockSpec((OWNERS, 1...]
where the time goes in v4:
time: 200 us
  Pallas kernels  148 us (74%)
  blocking collectives  50.8 us (25%)
    pallas_call x1, Pallas kernels, reduce_all(): pl.pallas_call(reduce_kernel, out_shape=tuple((jax.ShapeDtypeStruct((2048...  54.7 us
    all_to_all x2, blocking collectives, exchange(): return lax.all_to_all(x, AXES, split_axis=0, concat_axis=0, tiled=True)  50.8 us
    pallas_call x1, Pallas kernels, core_grads(): pl.pallas_call(core_grad_kernel, grid=(2,), in_specs=[pl.BlockSpec((OWNER...  22.7 us
    pallas_call x1, Pallas kernels, build(): pl.pallas_call(build_kernel, grid=(2,), in_specs=[pl.BlockSpec((OWNERS, 1...  22.6 us
    pallas_call x1, Pallas kernels, layer(): pl.pallas_call(layer_kernel, out_shape=(jax.ShapeDtypeStruct((EVENTS, 512...  22.3 us
    pallas_call x1, Pallas kernels, prep(): pl.pallas_call(prep_kernel, out_shape=(jax.ShapeDtypeStruct((16, 8, 1, 12...  17.6 us
    pallas_call x1, Pallas kernels, widen(): pl.pallas_call(widen_kernel, grid=(steps,), in_specs=[pl.BlockSpec((4 * r...  8.24 us

profile of v4, /device:TPU:1, one launch (start us, length us, event | category | flops | bytes accessed | tf_op | source)
XLA Modules:
  0.0 199.6 jit_solution(1507052224215383423)
XLA Ops:
  0.6 17.6 %prep.1 = (s32[16,8,1,128]{3,2,1,0:T(1,128)}, s32[8,512]{1,0:T(8,128)}, s32[512,128]{1,0:T(8,128)}) custom-call(s32[3,512]{1,0:T(4,128)} %dig_ref.1), custom_call_target="tpu_custom_call" | custom-call | tf_op jit(solution)/shard_map/prep/pallas_call | solution.py:105
  18.3 22.6 %build.1 = (bf16[128,2,16,128]{3,2,1,0:T(8,128)(2,1)}, bf16[8192,256]{1,0:T(8,128)(2,1)}, bf16[256,64,256]{2,1,0:T(8,128)(2,1)}, bf16[256,32,256]{2,1,0:T(8,128)(2,1)}) custom-call(s32[128,1,128]{2,1,0:T(1,128)} %bitcast.6, bf16[2048,512]{1,0:T(8,128)(2,1)} %first_ref.1, bf16[256,512]{1,0:T(8,128)(2,1)} %middle_ref.3, bf16[1024,512]{1,0:T(8,128)(2,1)} %last_ref.1), custom_call_target="tpu_custom_call" | custom-call | tf_op jit(solution)/shard_map/build/pallas_call | solution.py:215
  40.9 26.1 %all_to_all.10.recv_ref = bf16[128,2,16,128]{3,2,1,0:T(8,128)(2,1)} all-to-all(bf16[128,2,16,128]{3,2,1,0:T(8,128)(2,1)} %get-tuple-element.28), channel_id=1, replica_groups=mesh['dp'=16,'cores'=8] {'dp','cores'}, dimensions={0} | all-to-all | bytes 2097152 | tf_op jit(solution)/shard_map/all_to_all | solution.py:830
  67.0 22.3 %layer.1 = (bf16[512,512]{1,0:T(8,128)(2,1)}, bf16[128,2,16,128]{3,2,1,0:T(8,128)(2,1)}, bf16[2048,512]{1,0:T(8,128)(2,1)}, bf16[512,512]{1,0:T(8,128)(2,1)}) custom-call(bf16[128,2,16,128]{3,2,1,0:T(8,128)(2,1)} %all_to_all.10.recv_ref, s32[8,512]{1,0:T(8,128)} %get-tuple-element.29.slot_row_ref, s32[512,128]{1,0:T(8,128)} %get-tuple-element.30.slot_col_ref, ...), custom_call_target="tpu_custom_call" | custom-call | tf_op jit(solution)/shard_map/layer/pallas_call | solution.py:423
  89.2 24.7 %all_to_all.11.tile_ref = bf16[128,2,16,128]{3,2,1,0:T(8,128)(2,1)} all-to-all(bf16[128,2,16,128]{3,2,1,0:T(8,128)(2,1)} %get-tuple-element.32), channel_id=1, replica_groups=mesh['dp'=16,'cores'=8] {'dp','cores'}, dimensions={0} | all-to-all | bytes 2097152 | tf_op jit(solution)/shard_map/all_to_all | solution.py:830
  114.0 22.7 %core_grads.1 = (bf16[2048,512]{1,0:T(8,128)(2,1)}, f32[256,512]{1,0:T(8,128)}, bf16[1024,512]{1,0:T(8,128)(2,1)}) custom-call(s32[128,1,128]{2,1,0:T(1,128)} %bitcast.7, bf16[128,2,16,128]{3,2,1,0:T(8,128)(2,1)} %all_to_all.11.tile_ref, bf16[8192,256]{1,0:T(8,128)(2,1)} %get-tuple-element.33.spread_ref, bf16[256,64,256]{2,1,0:T(8,128)(2,1)} %get-tuple-element.34.part_ref, ...), custom_call_target="tpu_custom_call" | custom-call | tf_op jit(solution)/shard_map/core_grads/pallas_call | solution.py:555
  136.7 54.7 %reduce_all.1 = (bf16[2048,512]{1,0:T(8,128)(2,1)}, bf16[2048,512]{1,0:T(8,128)(2,1)}, bf16[2048,384]{1,0:T(8,128)(2,1)}) custom-call(bf16[2048,512]{1,0:T(8,128)(2,1)} %get-tuple-element.36.first_ref, bf16[2048,512]{1,0:T(8,128)(2,1)} %get-tuple-element.37.proj_ref, bf16[1024,512]{1,0:T(8,128)(2,1)} %get-tuple-element.38.last_ref, ...), custom_call_target="tpu_custom_call" | custom-call | tf_op jit(solution)/shard_map/reduce_all/pallas_call | solution.py:768
  191.3 8.2 %widen.1 = (f32[2048,512]{1,0:T(8,128)}, f32[2,512,512]{2,1,0:T(8,128)}, f32[512,2048]{1,0:T(8,128)}, f32[512,512]{1,0:T(8,128)}) custom-call(bf16[2048,512]{1,0:T(8,128)(2,1)} %get-tuple-element.40.a_ref, bf16[4,512,512]{2,1,0:T(8,128)(2,1)} %bitcast.4, bf16[4,512,384]{2,1,0:T(8,128)(2,1)} %bitcast.5), custom_call_target="tpu_custom_call" | custom-call | tf_op jit(solution)/shard_map/widen/pallas_call | solution.py:803

commit v5 on v4

--- a/solution.py
+++ b/solution.py
@@ -116,7 +116,7 @@
             pltpu.SemaphoreType.DMA((22,)),
         ],
         compiler_params=pltpu.CompilerParams(
-            collective_id=1, has_side_effects=True, vmem_limit_bytes=VMEM_LIMIT
+            collective_id=1, has_side_effects=True, vmem_limit_bytes=16 * 1024 * 1024
         ),
         name="prep",
     )(digits)
@@ -238,7 +238,7 @@
             pltpu.VMEM((4096, 512), F32),
             pltpu.VMEM((2, 2048, 128), F32),
         ],
-        compiler_params=pltpu.CompilerParams(vmem_limit_bytes=VMEM_LIMIT),
+        compiler_params=pltpu.CompilerParams(vmem_limit_bytes=46 * 1024 * 1024),
         name="build",
     )(arrived, first_core, middle_core, last_core)
 
@@ -446,7 +446,7 @@
             vm((EVENTS, 128), F32),
             vm((EVENTS, 128), F32),
         ],
-        compiler_params=pltpu.CompilerParams(vmem_limit_bytes=VMEM_LIMIT),
+        compiler_params=pltpu.CompilerParams(vmem_limit_bytes=34 * 1024 * 1024),
         name="layer",
     )(recv, slot_row, slot_col, w_proj, w_out, layer_grad)
 
@@ -581,7 +581,7 @@
             vm((1024, 512), BF),
             vm((1024, 512), BF),
         ],
-        compiler_params=pltpu.CompilerParams(vmem_limit_bytes=VMEM_LIMIT),
+        compiler_params=pltpu.CompilerParams(vmem_limit_bytes=46 * 1024 * 1024),
         name="core_grads",
     )(arrived, tiles, spread, part, lt, middle_core)
 
@@ -777,7 +777,7 @@
         + [vm((2, 128, w), BF) for w in widths]
         + [pltpu.SemaphoreType.DMA((3, 8, 4))] * 2,
         compiler_params=pltpu.CompilerParams(
-            collective_id=ident, has_side_effects=True, vmem_limit_bytes=VMEM_LIMIT
+            collective_id=ident, has_side_effects=True, vmem_limit_bytes=28 * 1024 * 1024
         ),
         name="reduce_all",
     )(first_part, proj_grad, last_part, out_grad)
@@ -820,7 +820,7 @@
             jax.ShapeDtypeStruct((512, 2048), F32),
             jax.ShapeDtypeStruct((512, 512), F32),
         ),
-        compiler_params=pltpu.CompilerParams(vmem_limit_bytes=VMEM_LIMIT),
+        compiler_params=pltpu.CompilerParams(vmem_limit_bytes=20 * 1024 * 1024),
         name="widen",
     )(a, b.reshape(4, 512, 512), c.reshape(4, 512, 384))
     return first, last.reshape(1024, 512), proj, out

time: 200 us -> 187 us (0.935)
  Pallas kernels: 148 us -> 132 us
  local copies, waits for them, and re-layouts: 0 us -> 4.46 us
    pallas_call x1, Pallas kernels: 54.7 us -> 49.6 us  [reduce_all(): pl.pallas_call(reduce_kernel, out_shape=tuple((jax.ShapeDtypeStruct((2048...]
    unnamed x0 -> x16, local copies, waits for them, and re-layouts: none -> 4.46 us
    pallas_call x1, Pallas kernels: 22.3 us -> 18.9 us  [layer(): pl.pallas_call(layer_kernel, out_shape=(jax.ShapeDtypeStruct((EVENTS, 512...]
    pallas_call x1, Pallas kernels: 8.24 us -> 5.21 us  [widen(): pl.pallas_call(widen_kernel, grid=(steps,), in_specs=[pl.BlockSpec((4 * r...]
    pallas_call x1, Pallas kernels: 22.6 us -> 20.5 us  [build(): pl.pallas_call(build_kernel, grid=(2,), in_specs=[pl.BlockSpec((OWNERS, 1...]
where the time goes in v5:
time: 187 us; the launch traced here: 186 us
  Pallas kernels  132 us (71%)
  blocking collectives  49.2 us (26%)
  local copies, waits for them, and re-layouts  4.46 us (2%)
    pallas_call x1, Pallas kernels, reduce_all(): pl.pallas_call(reduce_kernel, out_shape=tuple((jax.ShapeDtypeStruct((2048...  49.6 us
    all_to_all x2, blocking collectives, exchange(): return lax.all_to_all(x, AXES, split_axis=0, concat_axis=0, tiled=True)  49.2 us
    pallas_call x1, Pallas kernels, core_grads(): pl.pallas_call(core_grad_kernel, grid=(2,), in_specs=[pl.BlockSpec((OWNER...  21.6 us
    pallas_call x1, Pallas kernels, build(): pl.pallas_call(build_kernel, grid=(2,), in_specs=[pl.BlockSpec((OWNERS, 1...  20.5 us
    pallas_call x1, Pallas kernels, layer(): pl.pallas_call(layer_kernel, out_shape=(jax.ShapeDtypeStruct((EVENTS, 512...  18.9 us
    pallas_call x1, Pallas kernels, prep(): pl.pallas_call(prep_kernel, out_shape=(jax.ShapeDtypeStruct((16, 8, 1, 12...  16.2 us
    pallas_call x1, Pallas kernels, widen(): pl.pallas_call(widen_kernel, grid=(steps,), in_specs=[pl.BlockSpec((4 * r...  5.21 us
    unnamed x16, local copies, waits for them, and re-layouts  4.46 us

profile of v5, /device:TPU:1, one launch (start us, length us, event | category | flops | bytes accessed | tf_op | source)
XLA Modules:
  0.0 186.3 jit_solution(1321259207836137123)
XLA Ops:
  0.6 0.0 copy-start.7
  0.6 0.7 copy-done.7
  1.3 16.2 %prep.1 = (s32[16,8,1,128]{3,2,1,0:T(1,128)S(1)}, s32[8,512]{1,0:T(8,128)S(1)}, s32[512,128]{1,0:T(8,128)S(1)}) custom-call(s32[3,512]{1,0:T(4,128)S(1)} %copy-done.7), custom_call_target="tpu_custom_call" | custom-call | tf_op jit(solution)/shard_map/prep/pallas_call | solution.py:105
  17.5 0.0 copy-start
  17.5 1.6 copy-done
  19.1 0.0 copy-start.2
  19.1 0.9 copy-done.2
  20.0 0.0 copy-start.4
  20.0 1.2 copy-done.4
  21.3 0.0 copy-start.1
  21.3 0.0 copy-start.5
  21.3 0.0 copy-start.6
  21.3 20.5 %build.1 = (bf16[128,2,16,128]{3,2,1,0:T(8,128)(2,1)S(1)}, bf16[8192,256]{1,0:T(8,128)(2,1)}, bf16[256,64,256]{2,1,0:T(8,128)(2,1)}, bf16[256,32,256]{2,1,0:T(8,128)(2,1)}) custom-call(s32[128,1,128]{2,1,0:T(1,128)S(1)} %bitcast.6, bf16[2048,512]{1,0:T(8,128)(2,1)S(1)} %copy-done, bf16[256,512]{1,0:T(8,128)(2,1)S(1)} %copy-done.2, ...), custom_call_target="tpu_custom_call" | custom-call | tf_op jit(solution)/shard_map/build/pallas_call | solution.py:215
  41.7 25.7 %all_to_all.10.recv_ref = bf16[128,2,16,128]{3,2,1,0:T(8,128)(2,1)S(1)} all-to-all(bf16[128,2,16,128]{3,2,1,0:T(8,128)(2,1)S(1)} %get-tuple-element.28), channel_id=1, replica_groups=mesh['dp'=16,'cores'=8] {'dp','cores'}, dimensions={0} | all-to-all | bytes 2097152 | tf_op jit(solution)/shard_map/all_to_all | solution.py:830
  67.5 0.0 copy-done.1
  67.5 0.0 copy-done.5
  67.5 0.0 copy-done.6
  67.5 18.9 %layer.1 = (bf16[512,512]{1,0:T(8,128)(2,1)}, bf16[128,2,16,128]{3,2,1,0:T(8,128)(2,1)S(1)}, bf16[2048,512]{1,0:T(8,128)(2,1)S(1)}, bf16[512,512]{1,0:T(8,128)(2,1)S(1)}) custom-call(bf16[128,2,16,128]{3,2,1,0:T(8,128)(2,1)S(1)} %all_to_all.10.recv_ref, s32[8,512]{1,0:T(8,128)S(1)} %get-tuple-element.29.slot_row_ref, ...), custom_call_target="tpu_custom_call" | custom-call | tf_op jit(solution)/shard_map/layer/pallas_call | solution.py:423
  86.4 0.0 copy-start.3
  86.4 23.5 %all_to_all.11.tile_ref = bf16[128,2,16,128]{3,2,1,0:T(8,128)(2,1)S(1)} all-to-all(bf16[128,2,16,128]{3,2,1,0:T(8,128)(2,1)S(1)} %get-tuple-element.32), channel_id=1, replica_groups=mesh['dp'=16,'cores'=8] {'dp','cores'}, dimensions={0} | all-to-all | bytes 2097152 | tf_op jit(solution)/shard_map/all_to_all | solution.py:830
  109.9 0.0 copy-done.3
  109.9 21.6 %core_grads.1 = (bf16[2048,512]{1,0:T(8,128)(2,1)S(1)}, f32[256,512]{1,0:T(8,128)}, bf16[1024,512]{1,0:T(8,128)(2,1)S(1)}) custom-call(s32[128,1,128]{2,1,0:T(1,128)S(1)} %bitcast.7, bf16[128,2,16,128]{3,2,1,0:T(8,128)(2,1)S(1)} %all_to_all.11.tile_ref, bf16[8192,256]{1,0:T(8,128)(2,1)} %get-tuple-element.33.spread_ref, ...), custom_call_target="tpu_custom_call" | custom-call | tf_op jit(solution)/shard_map/core_grads/pallas_call | solution.py:555
  131.4 49.6 %reduce_all.1 = (bf16[2048,512]{1,0:T(8,128)(2,1)S(1)}, bf16[2048,512]{1,0:T(8,128)(2,1)S(1)}, bf16[2048,384]{1,0:T(8,128)(2,1)S(1)}) custom-call(bf16[2048,512]{1,0:T(8,128)(2,1)S(1)} %get-tuple-element.36.first_ref, bf16[2048,512]{1,0:T(8,128)(2,1)S(1)} %get-tuple-element.37.proj_ref, bf16[1024,512]{1,0:T(8,128)(2,1)S(1)} %get-tuple-element.38.last_ref, ...), custom_call_target="tpu_custom_call" | custom-call | tf_op jit(solution)/shard_map/reduce_all/pallas_call | solution.py:768
  181.0 5.2 %widen.1 = (f32[2048,512]{1,0:T(8,128)}, f32[2,512,512]{2,1,0:T(8,128)}, f32[512,2048]{1,0:T(8,128)}, f32[512,512]{1,0:T(8,128)}) custom-call(bf16[2048,512]{1,0:T(8,128)(2,1)S(1)} %get-tuple-element.40.a_ref, bf16[4,512,512]{2,1,0:T(8,128)(2,1)S(1)} %bitcast.4, bf16[4,512,384]{2,1,0:T(8,128)(2,1)S(1)} %bitcast.5), custom_call_target="tpu_custom_call" | custom-call | tf_op jit(solution)/shard_map/widen/pallas_call | solution.py:803
Async XLA Ops:
  0.6 0.7 copy-start.7
  17.5 1.6 copy-start
  19.1 0.9 copy-start.2
  20.0 1.2 copy-start.4
  21.3 46.2 %copy-start.1 = (bf16[512,2048]{1,0:T(8,128)(2,1)S(1)}, bf16[512,2048]{1,0:T(8,128)(2,1)}, u32[]{:S(2)}) copy-start(bf16[512,2048]{1,0:T(8,128)(2,1)} %proj_ref.1) | copy-start | bytes 6291460
  21.3 46.2 %copy-start.5 = (bf16[512,512]{1,0:T(8,128)(2,1)S(1)}, bf16[512,512]{1,0:T(8,128)(2,1)}, u32[]{:S(2)}) copy-start(bf16[512,512]{1,0:T(8,128)(2,1)} %out_ref.1) | copy-start | bytes 1572868
  21.3 46.2 %copy-start.6 = (bf16[512,512]{1,0:T(8,128)(2,1)S(1)}, bf16[512,512]{1,0:T(8,128)(2,1)}, u32[]{:S(2)}) copy-start(bf16[512,512]{1,0:T(8,128)(2,1)} %grad_ref.1) | copy-start | bytes 1572868
  86.4 23.5 %copy-start.3 = (bf16[256,512]{1,0:T(8,128)(2,1)S(1)}, bf16[256,512]{1,0:T(8,128)(2,1)}, u32[]{:S(2)}) copy-start(bf16[256,512]{1,0:T(8,128)(2,1)} %middle_ref.3) | copy-start | bytes 786436

commit v6 on v5

--- a/solution.py
+++ b/solution.py
@@ -467,6 +467,7 @@
 
     def events(i, carry):
         srcs = pl.ds(pl.multiple_of(i * group, group), group)
+        stored = pl.ds(pl.multiple_of(half * OWNERS + i * group, group), group)
         tile = tile_ref[srcs, 0]
         g = jnp.concatenate([tile[:, :, 0:64], tile[:, :, 64:128]], axis=1)
         wide = pl.ds(pl.multiple_of(i * group * 16, group * 16), group * 16)
@@ -475,7 +476,7 @@
             x = terms[:, side * 16 : (side + 1) * 16, side * 128 : (side + 1) * 128]
             x = jnp.where(own, x, 0.0).reshape(group * 16, 128)
             ls[side, wide, :] = x + half_turn(x)
-        grads = bdot(g, lt_ref[srcs], 1, 1)
+        grads = bdot(g, lt_ref[stored], 1, 1)
         for pair in range(4):
             lanes = slice(pair * 128, (pair + 1) * 128)
             for side in range(2):
@@ -493,7 +494,7 @@
     middle_part = jnp.zeros((256, 512), F32)
     for t in range(4):
         at = slice(t * 1024, (t + 1) * 1024)
-        middle_part += dot(spread_ref[at, :], pg[at, :], 0, 0)
+        middle_part += dot(spread_ref[pl.ds(pl.multiple_of(half * 4096 + t * 1024, 1024), 1024), :], pg[at, :], 0, 0)
         back = dot(pg[at, :], middle_ref[...], 1, 1)
         ss[0] = back[:, 0:128]
         ss[1] = back[:, 128:256]
@@ -558,9 +559,9 @@
         in_specs=[
             pl.BlockSpec((OWNERS, 1, 128), lambda h: (0, 0, 0)),
             pl.BlockSpec((OWNERS, 1, 16, 128), lambda h: (0, h, 0, 0)),
-            pl.BlockSpec((4096, 256), lambda h: (h, 0)),
+            pl.BlockSpec(memory_space=pltpu.VMEM),
             pl.BlockSpec((OWNERS, 64, 256), lambda h: (h, 0, 0)),
-            pl.BlockSpec((OWNERS, 32, 256), lambda h: (h, 0, 0)),
+            pl.BlockSpec(memory_space=pltpu.VMEM),
             pl.BlockSpec((256, 512), lambda h: (0, 0)),
         ],
         out_specs=(
@@ -581,7 +582,7 @@
             vm((1024, 512), BF),
             vm((1024, 512), BF),
         ],
-        compiler_params=pltpu.CompilerParams(vmem_limit_bytes=46 * 1024 * 1024),
+        compiler_params=pltpu.CompilerParams(vmem_limit_bytes=36 * 1024 * 1024),
         name="core_grads",
     )(arrived, tiles, spread, part, lt, middle_core)
 

time: 187 us -> 185 us (0.989)
    unnamed x16 -> x20, local copies, waits for them, and re-layouts: 4.46 us -> 4.47 us
where the time goes in v6:
time: 185 us
  Pallas kernels  131 us (71%)
  blocking collectives  49.2 us (27%)
  local copies, waits for them, and re-layouts  4.47 us (2%)
    pallas_call x1, Pallas kernels, reduce_all(): pl.pallas_call(reduce_kernel, out_shape=tuple((jax.ShapeDtypeStruct((2048...  49.6 us
    all_to_all x2, blocking collectives, exchange(): return lax.all_to_all(x, AXES, split_axis=0, concat_axis=0, tiled=True)  49.2 us
    pallas_call x1, Pallas kernels, build(): pl.pallas_call(build_kernel, grid=(2,), in_specs=[pl.BlockSpec((OWNERS, 1...  20.5 us
    pallas_call x1, Pallas kernels, core_grads(): pl.pallas_call(core_grad_kernel, grid=(2,), in_specs=[pl.BlockSpec((OWNER...  20.3 us
    pallas_call x1, Pallas kernels, layer(): pl.pallas_call(layer_kernel, out_shape=(jax.ShapeDtypeStruct((EVENTS, 512...  18.9 us
    pallas_call x1, Pallas kernels, prep(): pl.pallas_call(prep_kernel, out_shape=(jax.ShapeDtypeStruct((16, 8, 1, 12...  16.2 us
    pallas_call x1, Pallas kernels, widen(): pl.pallas_call(widen_kernel, grid=(steps,), in_specs=[pl.BlockSpec((4 * r...  5.21 us
    unnamed x20, local copies, waits for them, and re-layouts  4.47 us

profile of v6, /device:TPU:1, one launch (start us, length us, event | category | flops | bytes accessed | tf_op | source)
XLA Modules:
  0.0 185.0 jit_solution(9292998097215666491)
XLA Ops:
  0.6 0.0 copy-start.9
  0.6 0.7 copy-done.9
  1.3 16.2 %prep.1 = (s32[16,8,1,128]{3,2,1,0:T(1,128)S(1)}, s32[8,512]{1,0:T(8,128)S(1)}, s32[512,128]{1,0:T(8,128)S(1)}) custom-call(s32[3,512]{1,0:T(4,128)S(1)} %copy-done.9), custom_call_target="tpu_custom_call" | custom-call | tf_op jit(solution)/shard_map/prep/pallas_call | solution.py:105
  17.5 0.0 copy-start.2
  17.5 1.6 copy-done.2
  19.1 0.0 copy-start.4
  19.1 0.9 copy-done.4
  20.0 0.0 copy-start.6
  20.0 1.2 copy-done.6
  21.3 0.0 copy-start.3
  21.3 0.0 copy-start.7
  21.3 0.0 copy-start.8
  21.3 20.5 %build.1 = (bf16[128,2,16,128]{3,2,1,0:T(8,128)(2,1)S(1)}, bf16[8192,256]{1,0:T(8,128)(2,1)}, bf16[256,64,256]{2,1,0:T(8,128)(2,1)}, bf16[256,32,256]{2,1,0:T(8,128)(2,1)}) custom-call(s32[128,1,128]{2,1,0:T(1,128)S(1)} %bitcast.6, bf16[2048,512]{1,0:T(8,128)(2,1)S(1)} %copy-done.2, bf16[256,512]{1,0:T(8,128)(2,1)S(1)} %copy-done.4, ...), custom_call_target="tpu_custom_call" | custom-call | tf_op jit(solution)/shard_map/build/pallas_call | solution.py:215
  41.7 0.0 copy-start.1
  41.7 25.7 %all_to_all.10.recv_ref = bf16[128,2,16,128]{3,2,1,0:T(8,128)(2,1)S(1)} all-to-all(bf16[128,2,16,128]{3,2,1,0:T(8,128)(2,1)S(1)} %get-tuple-element.28), channel_id=1, replica_groups=mesh['dp'=16,'cores'=8] {'dp','cores'}, dimensions={0} | all-to-all | bytes 2097152 | tf_op jit(solution)/shard_map/all_to_all | solution.py:831
  67.5 0.0 copy-done.3
  67.5 0.0 copy-done.7
  67.5 0.0 copy-done.8
  67.5 0.0 copy-start
  67.5 18.9 %layer.1 = (bf16[512,512]{1,0:T(8,128)(2,1)}, bf16[128,2,16,128]{3,2,1,0:T(8,128)(2,1)S(1)}, bf16[2048,512]{1,0:T(8,128)(2,1)S(1)}, bf16[512,512]{1,0:T(8,128)(2,1)S(1)}) custom-call(bf16[128,2,16,128]{3,2,1,0:T(8,128)(2,1)S(1)} %all_to_all.10.recv_ref, s32[8,512]{1,0:T(8,128)S(1)} %get-tuple-element.29.slot_row_ref, ...), custom_call_target="tpu_custom_call" | custom-call | tf_op jit(solution)/shard_map/layer/pallas_call | solution.py:423
  86.4 0.0 copy-start.5
  86.4 23.5 %all_to_all.11.tile_ref = bf16[128,2,16,128]{3,2,1,0:T(8,128)(2,1)S(1)} all-to-all(bf16[128,2,16,128]{3,2,1,0:T(8,128)(2,1)S(1)} %get-tuple-element.32), channel_id=1, replica_groups=mesh['dp'=16,'cores'=8] {'dp','cores'}, dimensions={0} | all-to-all | bytes 2097152 | tf_op jit(solution)/shard_map/all_to_all | solution.py:831
  109.9 0.0 copy-done.1
  109.9 0.0 copy-done
  109.9 0.0 copy-done.5
  109.9 20.3 %core_grads.1 = (bf16[2048,512]{1,0:T(8,128)(2,1)S(1)}, f32[256,512]{1,0:T(8,128)}, bf16[1024,512]{1,0:T(8,128)(2,1)S(1)}) custom-call(s32[128,1,128]{2,1,0:T(1,128)S(1)} %bitcast.7, bf16[128,2,16,128]{3,2,1,0:T(8,128)(2,1)S(1)} %all_to_all.11.tile_ref, bf16[8192,256]{1,0:T(8,128)(2,1)S(1)} %copy-done, bf16[256,64,256]{2,1,0:T(8,128)(2,1)} %get-tuple-element.34.part_ref, ...), custom_call_target="tpu_custom_call" | custom-call | tf_op jit(solution)/shard_map/core_grads/pallas_call | solution.py:556
  130.2 49.6 %reduce_all.1 = (bf16[2048,512]{1,0:T(8,128)(2,1)S(1)}, bf16[2048,512]{1,0:T(8,128)(2,1)S(1)}, bf16[2048,384]{1,0:T(8,128)(2,1)S(1)}) custom-call(bf16[2048,512]{1,0:T(8,128)(2,1)S(1)} %get-tuple-element.36.first_ref, bf16[2048,512]{1,0:T(8,128)(2,1)S(1)} %get-tuple-element.37.proj_ref, bf16[1024,512]{1,0:T(8,128)(2,1)S(1)} %get-tuple-element.38.last_ref, ...), custom_call_target="tpu_custom_call" | custom-call | tf_op jit(solution)/shard_map/reduce_all/pallas_call | solution.py:769
  179.8 5.2 %widen.1 = (f32[2048,512]{1,0:T(8,128)}, f32[2,512,512]{2,1,0:T(8,128)}, f32[512,2048]{1,0:T(8,128)}, f32[512,512]{1,0:T(8,128)}) custom-call(bf16[2048,512]{1,0:T(8,128)(2,1)S(1)} %get-tuple-element.40.a_ref, bf16[4,512,512]{2,1,0:T(8,128)(2,1)S(1)} %bitcast.4, bf16[4,512,384]{2,1,0:T(8,128)(2,1)S(1)} %bitcast.5), custom_call_target="tpu_custom_call" | custom-call | tf_op jit(solution)/shard_map/widen/pallas_call | solution.py:804
Async XLA Ops:
  0.6 0.7 copy-start.9
  17.5 1.6 copy-start.2
  19.1 0.9 copy-start.4
  20.0 1.2 copy-start.6
  21.3 46.2 %copy-start.3 = (bf16[512,2048]{1,0:T(8,128)(2,1)S(1)}, bf16[512,2048]{1,0:T(8,128)(2,1)}, u32[]{:S(2)}) copy-start(bf16[512,2048]{1,0:T(8,128)(2,1)} %proj_ref.1) | copy-start | bytes 6291460
  21.3 46.2 %copy-start.7 = (bf16[512,512]{1,0:T(8,128)(2,1)S(1)}, bf16[512,512]{1,0:T(8,128)(2,1)}, u32[]{:S(2)}) copy-start(bf16[512,512]{1,0:T(8,128)(2,1)} %out_ref.1) | copy-start | bytes 1572868
  21.3 46.2 %copy-start.8 = (bf16[512,512]{1,0:T(8,128)(2,1)S(1)}, bf16[512,512]{1,0:T(8,128)(2,1)}, u32[]{:S(2)}) copy-start(bf16[512,512]{1,0:T(8,128)(2,1)} %grad_ref.1) | copy-start | bytes 1572868
  41.7 68.1 %copy-start.1 = (bf16[256,32,256]{2,1,0:T(8,128)(2,1)S(1)}, bf16[256,32,256]{2,1,0:T(8,128)(2,1)}, u32[]{:S(2)}) copy-start(bf16[256,32,256]{2,1,0:T(8,128)(2,1)} %get-tuple-element.35.lt_ref) | copy-start | bytes 12582916
  67.5 42.4 %copy-start = (bf16[8192,256]{1,0:T(8,128)(2,1)S(1)}, bf16[8192,256]{1,0:T(8,128)(2,1)}, u32[]{:S(2)}) copy-start(bf16[8192,256]{1,0:T(8,128)(2,1)} %get-tuple-element.33.spread_ref) | copy-start | bytes 12582916
  86.4 23.5 %copy-start.5 = (bf16[256,512]{1,0:T(8,128)(2,1)S(1)}, bf16[256,512]{1,0:T(8,128)(2,1)}, u32[]{:S(2)}) copy-start(bf16[256,512]{1,0:T(8,128)(2,1)} %middle_ref.3) | copy-start | bytes 786436
